TPU v7x, 256 devices: a whole 4x4x8 slice. The times are simulated.
256 devices in a mesh: dp: 64 (over x, y, z_lo, core), fsdp: 4 (over z_hi).
Axes of the slice: x: 4, y: 4, z: 8 (z_hi: 4, z_lo: 2; z = z_hi * 2 + z_lo), core: 2. Of those that a mesh axis runs over, the one named last changes fastest.
Arguments:
- step_index: int32 [1], replicated, may hold values from 0 to 999
- token_codes: int32 [64, 1024], P('dp', 'fsdp'), may hold values from 0 to 65535
- params: bfloat16 [64, 2560, 2560], P('dp', 'fsdp'), may hold values from -0.125 to 0.125
- moments: bfloat16 [64, 2560, 2560], P('dp', 'fsdp'), may hold values from -6 to 6
- second: float32 [64, 2560], P('dp', 'fsdp'), may hold values from 0.5 to 50
Outputs:
- new_params: bfloat16 [64, 2560, 2560], P('dp', 'fsdp')
- new_moments: bfloat16 [64, 2560, 2560], P('dp', 'fsdp')
- new_second: float32 [64, 2560], P('dp', 'fsdp')
All inputs are finite; a program needn't handle non-finite values.
Results may differ from a plain program's by a relative error of at most 0.012.
Values may be sent and summed in bfloat16 or wider, within the bound.
No kernel may reach another device: no remote copies, remote signals or barrier semaphores. Data moves between devices by JAX's collectives and lax.ppermute only.
A program may use at most 128 MiB of HBM per device.

v0:
```python
from functools import partial
import math

import jax
import jax.numpy as jnp
from jax import lax
from jax.experimental import pallas as pl
from jax.experimental.pallas import tpu as pltpu
from jax.sharding import PartitionSpec as P

GELU_SCALE = math.sqrt(2.0 / math.pi)
GELU_CUBIC = 0.044715
BETA_ONE = 0.9
BETA_TWO = 0.999
LEARN_RATE = 0.001
EPSILON = 1e-08
LANES = 128
BAND = 16


def turn_pair(turns):
    quarter = (turns + 8192) >> 14
    rest = (turns - (quarter << 14)).astype(jnp.float32) * (2.0 * math.pi / 65536.0)
    square = rest * rest
    sine = rest + rest * square * (
        -1.6666654611e-1 + square * (8.3321608736e-3 + square * -1.9515295891e-4)
    )
    cosine = (
        1.0
        - 0.5 * square
        + square * square * (4.166664568298827e-2 + square * (-1.388731625493765e-3 + square * 2.443315711809948e-5))
    )
    odd = (quarter & 1) == 1
    cos_size = jnp.where(odd, sine, cosine)
    sin_size = jnp.where(odd, cosine, sine)
    cos_minus = ((quarter + 1) & 2) == 2
    sin_minus = (quarter & 2) == 2
    return (jnp.where(cos_minus, -cos_size, cos_size), jnp.where(sin_minus, -sin_size, sin_size))


def features_kernel(first_ref, codes_ref, feats_ref, change_ref, near_ref, far_ref, band_ref, block_ref):
    tokens, width_all = feats_ref.shape
    own_rows = change_ref.shape[0]
    root = math.sqrt(2.0)
    row = jnp.broadcast_to(codes_ref[...], (LANES, tokens))

    code = row.T
    step = (2 * code + 977) & 65535
    lane = lax.broadcasted_iota(jnp.int32, (tokens, LANES), 1)
    near_ref[0], near_ref[1] = turn_pair((step * lane) & 65535)
    far_cos, far_sin = turn_pair((code + step * (lane * LANES)) & 65535)
    far_ref[0], far_ref[1] = far_cos * root, far_sin * root

    def some_tokens(k, _):
        rows = pl.ds(k * 32, 32)
        near_cos, near_sin = near_ref[0, rows, :], near_ref[1, rows, :]
        far_cos, far_sin = far_ref[0, rows, :], far_ref[1, rows, :]
        for a in range(width_all // LANES):
            feats_ref[rows, a * LANES : (a + 1) * LANES] = (
                far_cos[:, a : a + 1] * near_cos - far_sin[:, a : a + 1] * near_sin
            ).astype(feats_ref.dtype)
        return 0

    lax.fori_loop(0, tokens // 32, some_tokens, 0)

    blocks = own_rows // BAND
    band = lax.broadcasted_iota(jnp.int32, (BAND, tokens), 0)
    block = lax.broadcasted_iota(jnp.int32, (blocks, tokens), 0)
    step = (2 * row + 977) & 65535
    near_cos, near_sin = turn_pair((step[:BAND] * band) & 65535)
    far_cos, far_sin = turn_pair((row[:blocks] + step[:blocks] * (first_ref[0] + block * BAND)) & 65535)
    for k, value in enumerate((near_cos, near_sin)):
        band_ref[k], band_ref[2 + k] = value, pltpu.roll(value, tokens - 1, 1)
    for k, value in enumerate((far_cos * root, far_sin * root)):
        block_ref[k], block_ref[2 + k] = value, pltpu.roll(value, tokens - 1, 1)

    def some_rows(a, _):
        one = pl.ds(a, 1)
        here, there = (
            (block_ref[k, one, :] * band_ref[k] - block_ref[k + 1, one, :] * band_ref[k + 1])
            .astype(feats_ref.dtype)
            .astype(jnp.float32)
            for k in (0, 2)
        )
        change_ref[pl.ds(pl.multiple_of(a * BAND, BAND), BAND), :] = here - there
        return 0

    lax.fori_loop(0, blocks, some_rows, 0, unroll=4)


def make_features(codes, first_col, tok_rows, own_rows, width_all):
    count = codes.shape[0]
    return pl.pallas_call(
        features_kernel,
        grid=(count,),
        out_shape=(
            jax.ShapeDtypeStruct((count * tok_rows, width_all), jnp.bfloat16),
            jax.ShapeDtypeStruct((own_rows, count * tok_rows), jnp.float32),
        ),
        in_specs=[
            pl.BlockSpec(memory_space=pltpu.SMEM),
            pl.BlockSpec((None, 1, tok_rows), lambda s: (s, 0, 0)),
        ],
        out_specs=(
            pl.BlockSpec((tok_rows, width_all), lambda s: (s, 0)),
            pl.BlockSpec((own_rows, tok_rows), lambda s: (0, s)),
        ),
        scratch_shapes=[
            pltpu.VMEM((2, tok_rows, LANES), jnp.float32),
            pltpu.VMEM((2, tok_rows, LANES), jnp.float32),
            pltpu.VMEM((4, BAND, tok_rows), jnp.float32),
            pltpu.VMEM((4, own_rows // BAND, tok_rows), jnp.float32),
        ],
        compiler_params=pltpu.CompilerParams(vmem_limit_bytes=32 * 2**20),
        cost_estimate=pl.CostEstimate(
            flops=12 * 10**9, bytes_accessed=8 * 2**20, transcendentals=0
        ),
    )(first_col.reshape(1), codes[:, None, :])


def gradient_kernel(order, own_ref, far_ref, feats_ref, change_ref, mom_ref, second_ref, mixed_ref, lead_ref, *refs):
    new_ref, rate_ref = refs[:2][::order]
    error_ref, column_ref = refs[2:]
    sequence = pl.program_id(0)
    own_rows, width_all = own_ref.shape
    tokens = feats_ref.shape[0]

    @pl.when(sequence == 0)
    def _():
        def mix(k, _):
            rows = pl.ds(pl.multiple_of(k * 16, 16), 16)
            mixed_ref[rows, :] = (
                0.5 * (own_ref[rows, :].astype(jnp.float32) + far_ref[rows, :].astype(jnp.float32))
            ).astype(mixed_ref.dtype)
            lead_ref[rows, :] = jnp.zeros((16, width_all), jnp.float32)
            return 0

        lax.fori_loop(0, own_rows // 16, mix, 0)

    half = own_rows // 2

    def forward(k, _):
        rows = pl.ds(pl.multiple_of(k * half, half), half)
        hidden = lax.dot_general(
            mixed_ref[rows, :], feats_ref[...], (((1,), (1,)), ((), ())), preferred_element_type=jnp.float32
        )
        squared = hidden * hidden
        tangent = jnp.tanh(GELU_SCALE * hidden * (1.0 + GELU_CUBIC * squared))
        value = 0.5 * hidden * (1.0 + tangent)
        slope = 0.5 * (1.0 + tangent) + 0.5 * hidden * (1.0 - tangent * tangent) * GELU_SCALE * (
            1.0 + 3.0 * GELU_CUBIC * squared
        )
        keep = lax.broadcasted_iota(jnp.int32, (half, tokens), 1) < tokens - 1
        error_ref[rows, :] = jnp.where(keep, (change_ref[rows, :] + value) * slope, 0.0).astype(
            error_ref.dtype
        )
        return 0

    lax.fori_loop(0, 2, forward, 0)

    def backward(k, _):
        cut = pl.ds(pl.multiple_of(k * 256, 256), 256)
        term = lax.dot_general(
            error_ref[...], feats_ref[:, cut], (((1,), (0,)), ((), ())), preferred_element_type=jnp.float32
        )
        term = term.astype(jnp.bfloat16).astype(jnp.float32)
        lead_ref[:, cut] = lead_ref[:, cut] + term
        return 0

    lax.fori_loop(0, width_all // 256, backward, 0)

    @pl.when(sequence == pl.num_programs(0) - 1)
    def _():
        def finish(k, _):
            rows = pl.ds(pl.multiple_of(k * 16, 16), 16)
            sums = jnp.zeros((16, LANES), jnp.float32)
            for low in range(0, width_all, LANES):
                grad = lead_ref[rows, low : low + LANES]
                sums += grad * grad
                lead_ref[rows, low : low + LANES] = (0.5 * BETA_ONE) * mom_ref[
                    rows, low : low + LANES
                ].astype(jnp.float32) + (1.0 - BETA_ONE) * grad
            column_ref[rows, :] = sums
            return 0

        lax.fori_loop(0, own_rows // 16, finish, 0)
        mean = jnp.sum(column_ref[...].T, axis=0, keepdims=True) / width_all
        second_new = BETA_TWO * second_ref[...] + (1.0 - BETA_TWO) * mean
        new_ref[...] = second_new
        rate = LEARN_RATE / (jnp.sqrt(second_new) + EPSILON)
        rate_ref[...] = jnp.broadcast_to(rate, (LANES, own_rows)).T[:, :1]


def make_gradient(own, far, feats, change, mom_own, second, tok_rows, order):
    own_rows, width_all = own.shape
    groups = feats.shape[0] // tok_rows

    shapes = (own.shape, own.shape) + ((1, own_rows), (own_rows, 1))[::order]
    types = (jnp.bfloat16, jnp.float32, jnp.float32, jnp.float32)

    def whole(shape):
        return pl.BlockSpec(shape, lambda s: (0, 0), pipeline_mode=pl.Buffered(1))

    return pl.pallas_call(
        partial(gradient_kernel, order),
        grid=(groups,),
        out_shape=tuple(jax.ShapeDtypeStruct(s, t) for s, t in zip(shapes, types)),
        in_specs=[
            whole(own.shape),
            whole(own.shape),
            pl.BlockSpec((tok_rows, width_all), lambda s: (s, 0)),
            pl.BlockSpec((own_rows, tok_rows), lambda s: (0, s)),
            whole(own.shape),
            whole((1, own_rows)),
        ],
        out_specs=tuple(whole(s) for s in shapes),
        scratch_shapes=[
            pltpu.VMEM((own_rows, tok_rows), jnp.bfloat16),
            pltpu.VMEM((own_rows, LANES), jnp.float32),
        ],
        compiler_params=pltpu.CompilerParams(vmem_limit_bytes=48 * 2**20),
        cost_estimate=pl.CostEstimate(
            flops=30 * 10**9,
            bytes_accessed=30 * 2**20,
            transcendentals=feats.shape[0] * own_rows,
        ),
    )(own, far, feats, change, mom_own, second)


def update_kernel(order, far_ref, lead_ref, mixed_ref, rate_ref, *refs):
    param_ref, mom_ref = refs[-2:][::order]

    def some_rows(k, _):
        rows = pl.ds(pl.multiple_of(k * 16, 16), 16)
        full = lead_ref[rows, :] + (0.5 * BETA_ONE) * far_ref[rows, :].astype(jnp.float32)
        mom_ref[rows, :] = full.astype(mom_ref.dtype)
        param_ref[rows, :] = (
            mixed_ref[rows, :].astype(jnp.float32) - rate_ref[rows, :] * full
        ).astype(param_ref.dtype)
        return 0

    lax.fori_loop(0, far_ref.shape[0] // 16, some_rows, 0)


def update(first, far, lead, mixed, rate, before, order):
    rows, width_all = far.shape
    block = max(b for b in range(16, 161, 16) if rows % b == 0 and first % b == 0)
    skip = first // block

    def cut(width, skip=skip):
        return pl.BlockSpec((block, width), lambda i: (skip + i, 0))

    whole = jax.ShapeDtypeStruct(lead.shape, jnp.bfloat16)
    held = () if before is None else tuple(before)
    return pl.pallas_call(
        partial(update_kernel, order),
        grid=(rows // block,),
        out_shape=(whole, whole),
        in_specs=[cut(width_all, 0), cut(width_all), cut(width_all), cut(1)]
        + [pl.BlockSpec(memory_space=pl.ANY)] * len(held),
        out_specs=(cut(width_all), cut(width_all)),
        input_output_aliases={4 + k: k for k in range(len(held))},
        compiler_params=pltpu.CompilerParams(vmem_limit_bytes=32 * 2**20),
        cost_estimate=pl.CostEstimate(
            flops=6 * rows * width_all, bytes_accessed=12 * rows * width_all, transcendentals=0
        ),
    )(far, lead, mixed, rate, *held)


def turned(value, axis, by):
    size = lax.axis_size(axis)
    return lax.ppermute(value, axis, [(i, (i + by) % size) for i in range(size)])


def long_way(distance, size):
    hops = []
    for hop in range(3):
        pairs = []
        for i in range(size):
            ring, place = i // (4 * distance), i // distance % 4
            began = (place + hop) % 4
            carry = 1 if hop == 1 and began == 3 else 0
            there = (ring + carry) * 4 * distance + (place - 1) % 4 * distance + i % distance
            pairs.append((i, there % size))
        hops.append(pairs)
    return hops


def step_at(token_codes, params, moments, second, distance):
    order = -1 if distance == 1 else 1
    groups = lax.axis_size("fsdp")
    tok_rows = token_codes.shape[1]
    own_rows, width_all = params.shape[1:]
    weights, mom_own = params[0], moments[0]

    weights_far = turned(weights, "dp", distance)
    if distance <= 2:
        codes = jnp.concatenate(
            [token_codes] + [turned(token_codes, "fsdp", k) for k in range(1, groups)]
        )
    else:
        codes = lax.all_to_all(
            jnp.broadcast_to(token_codes, (groups, tok_rows)), "fsdp", 0, 0, tiled=True
        )
    first_col = lax.axis_index("fsdp") * own_rows
    relay = distance in (4, 16)
    if relay:
        starts = (0, own_rows * 9 // 20, own_rows * 3 // 4, own_rows)
    else:
        starts = (0, own_rows * 4 // 5, own_rows)
    mom_far = []
    feats, change = make_features(codes, first_col, tok_rows, own_rows, width_all)
    if relay:
        first, second_hop, last = long_way(distance, lax.axis_size("dp"))
        relayed = lax.ppermute(mom_own[: starts[1]], "dp", first)
        relayed = lax.ppermute(relayed, "dp", second_hop)
        relayed, feats, change = lax.optimization_barrier((relayed, feats, change))
        mom_far.append(lax.ppermute(relayed, "dp", last))
    done = len(mom_far)
    for low, high in zip(starts[done:], starts[done + 1 :]):
        mom_far.append(turned(mom_own[low:high], "dp", distance))

    mixed, lead, *columns = make_gradient(
        weights, weights_far, feats, change, mom_own, second, tok_rows, order
    )
    second_new, rate = columns[::order]
    outs = None
    for low, far in zip(starts, mom_far):
        outs = update(low, far, lead, mixed, rate, outs, order)
    param_new, mom_new = outs[::order]
    return (param_new[None], mom_new[None], second_new)


def local(step_index, token_codes, params, moments, second):
    levels = min(5, lax.axis_size("dp").bit_length() - 1)
    branches = [partial(step_at, distance=2**power) for power in range(levels)]
    return lax.switch(step_index[0] % levels, branches, token_codes, params, moments, second)


def solution(mesh):
    in_specs = (P(), P("dp", "fsdp"), P("dp", "fsdp", None), P("dp", "fsdp", None), P("dp", "fsdp"))
    out_specs = (P("dp", "fsdp", None), P("dp", "fsdp", None), P("dp", "fsdp"))
    return jax.shard_map(local, mesh=mesh, in_specs=in_specs, out_specs=out_specs, check_vma=False)
```

profile of v0, /device:TPU:32, one launch (start us, length us, event | category | flops | bytes accessed | tf_op | source)
XLA Modules:
  0.0 150.0 jit_solution(12892291449438605565)
XLA Ops:
  1.3 148.7 %conditional.1 = (f32[1,640]{1,0:T(1,128)}, bf16[640,2560]{1,0:T(8,128)(2,1)}, bf16[640,2560]{1,0:T(8,128)(2,1)}) conditional(s32[]{:T(128)} %clamp.3, (bf16[1,640,2560]{2,1,0:T(8,128)(2,1)}, bf16[1,640,2560]{2,1,0:T(8,128)(2,1)}, s32[1,256]{1,0:T(1,128)}, f32[1,640]{1,0:T(1,128)}) %tuple.29, ...), branch_computations={%region_0.1_spmd, %region_1.2_spmd, %region_2.3_spmd, %region_3.4_... | conditional | flops 42009833472 | bytes 151285152 | solution.py:337
  1.5 3.3 %collective-permute-start.19 = (bf16[640,2560]{1,0:T(8,128)(2,1)}, bf16[640,2560]{1,0:T(8,128)(2,1)}, u32[]{:S(2)}, u32[]{:S(2)}) collective-permute-start(bf16[640,2560]{1,0:T(8,128)(2,1)} %bitcast.59), channel_id=1, source_target_pairs={{0,32},{4,36},{8,40},{12,44},{16,48},{20,52},{24,56},{28,60},{32,6... | collective-permute-start | bytes 9830408 | tf_op jit(solution)/shard_map/cond/branch_3_fun/ppermute | solution.py:272
  4.8 1.3 broadcast_in_dim.53
  6.1 7.6 %all-to-all-start.1 = ((s32[4,1,256]{2,1,0:T(1,128)}), s32[4,1,256]{2,1,0:T(1,128)S(1)}, u32[]{:S(2)}, u32[]{:S(2)}) async-start(s32[4,1,256]{2,1,0:T(1,128)} %broadcast_in_dim.53), calls=%async_computation.1 | async-start | bytes 8192 | tf_op jit(solution)/shard_map/cond/branch_3_fun/all_to_all | solution.py:302
  13.6 3.4 %slice_bitcast_fusion.7 = bf16[512,2560]{1,0:T(8,128)(2,1)} fusion(bf16[1,640,2560]{2,1,0:T(8,128)(2,1)} %get-tuple-element.87), kind=kLoop, calls=%fused_computation.9 | loop fusion | bytes 5242880 | tf_op jit(solution)/shard_map/cond/branch_3_fun/slice | solution.py:321
  17.0 1.3 collective-permute-start.20
  18.3 2.0 %slice_bitcast_fusion.8 = bf16[128,2560]{1,0:T(8,128)(2,1)} fusion(bf16[1,640,2560]{2,1,0:T(8,128)(2,1)} %get-tuple-element.87), kind=kLoop, calls=%fused_computation.10 | loop fusion | bytes 1310720 | tf_op jit(solution)/shard_map/cond/branch_3_fun/slice | solution.py:321
  20.3 3.2 %collective-permute-start.18 = (bf16[128,2560]{1,0:T(8,128)(2,1)}, bf16[128,2560]{1,0:T(8,128)(2,1)S(1)}, u32[]{:S(2)}, u32[]{:S(2)}) collective-permute-start(bf16[128,2560]{1,0:T(8,128)(2,1)} %slice_bitcast_fusion.8), channel_id=1, source_target_pairs={{0,32},{4,36},{8,40},{12,44},{16,48},{20,52},{24,56},{28,60},{32,6... | collective-permute-start | bytes 1966088 | tf_op jit(solution)/shard_map/cond/branch_3_fun/ppermute | solution.py:272
  23.5 0.0 all-to-all-done.1.codes_ref
  23.5 0.0 copy-start.15
  23.5 12.3 %branch_3_fun.4 = (bf16[1024,2560]{1,0:T(8,128)(2,1)S(1)}, f32[640,1024]{1,0:T(8,128)S(1)}) custom-call(s32[1]{0:T(128)} %bitcast.18.first_ref, s32[4,1,256]{2,1,0:T(1,128)S(1)} %all-to-all-done.1.codes_ref), custom_call_target="tpu_custom_call" | custom-call | flops 12000000000 | bytes 8388608 | tf_op jit(solution)/shard_map/cond/branch_3_fun/pallas_call | solution.py:93
  35.8 0.0 copy-start.9
  35.8 2.3 %copy-done.9 = bf16[1024,2560]{1,0:T(8,128)(2,1)} copy-done((bf16[1024,2560]{1,0:T(8,128)(2,1)}, bf16[1024,2560]{1,0:T(8,128)(2,1)S(1)}, u32[]{:S(2)}) %copy-start.9) | copy-done | bytes 5242904 | tf_op jit(solution)/shard_map/cond
  38.1 41.2 %collective-permute-done.19.far_ref = bf16[640,2560]{1,0:T(8,128)(2,1)} collective-permute-done((bf16[640,2560]{1,0:T(8,128)(2,1)}, bf16[640,2560]{1,0:T(8,128)(2,1)}, u32[]{:S(2)}, u32[]{:S(2)}) %collective-permute-start.19) | collective-permute-done | bytes 3276832 | tf_op jit(solution)/shard_map/cond/branch_3_fun/ppermute | solution.py:272
  79.3 0.0 copy-done.15
  79.3 26.3 %branch_3_fun.5 = (bf16[640,2560]{1,0:T(8,128)(2,1)S(1)}, f32[640,2560]{1,0:T(8,128)}, f32[1,640]{1,0:T(1,128)}, f32[640,1]{1,0:T(8,128)S(1)}) custom-call(bf16[640,2560]{1,0:T(8,128)(2,1)} %bitcast.60, bf16[640,2560]{1,0:T(8,128)(2,1)} %collective-permute-done.19.far_ref, bf16[1024,2560]{1,0:T(8,128)(2,1)} %copy-done.9, ...), custom_call_target="tpu_custom_call" | custom-call | flops 30000001024 | bytes 31457280 | tf_op jit(solution)/shard_map/cond/branch_3_fun/pallas_call | solution.py:204
  105.6 29.7 %collective-permute-done.20.far_ref = bf16[512,2560]{1,0:T(8,128)(2,1)S(1)} collective-permute-done((bf16[512,2560]{1,0:T(8,128)(2,1)}, bf16[512,2560]{1,0:T(8,128)(2,1)S(1)}, u32[]{:S(2)}, u32[]{:S(2)}) %collective-permute-start.20) | collective-permute-done | bytes 2621472 | tf_op jit(solution)/shard_map/cond/branch_3_fun/ppermute | solution.py:272
  135.4 0.0 copy-start.4
  135.4 2.9 %copy-done.4 = f32[640,2560]{1,0:T(8,128)S(1)} copy-done((f32[640,2560]{1,0:T(8,128)S(1)}, f32[640,2560]{1,0:T(8,128)}, u32[]{:S(2)}) %copy-start.4) | copy-done | bytes 6553624 | tf_op jit(solution)/shard_map/cond
  138.2 4.3 %branch_3_fun.6 = (bf16[640,2560]{1,0:T(8,128)(2,1)}, bf16[640,2560]{1,0:T(8,128)(2,1)}) custom-call(bf16[512,2560]{1,0:T(8,128)(2,1)S(1)} %collective-permute-done.20.far_ref, f32[640,2560]{1,0:T(8,128)S(1)} %copy-done.4, bf16[640,2560]{1,0:T(8,128)(2,1)S(1)} %get-tuple-element.94.mixed_ref, f32[640,1]{1,0:T(8,128)S(1)} %get-tuple-element.95.rate_ref), custom_call_target="tpu_custom_call" | custom-call | flops 7864320 | bytes 15728640 | tf_op jit(solution)/shard_map/cond/branch_3_fun/pallas_call | solution.py:255
  142.6 5.8 %collective-permute-done.18.far_ref = bf16[128,2560]{1,0:T(8,128)(2,1)S(1)} collective-permute-done((bf16[128,2560]{1,0:T(8,128)(2,1)}, bf16[128,2560]{1,0:T(8,128)(2,1)S(1)}, u32[]{:S(2)}, u32[]{:S(2)}) %collective-permute-start.18) | collective-permute-done | bytes 655392 | tf_op jit(solution)/shard_map/cond/branch_3_fun/ppermute | solution.py:272
  148.3 1.7 %branch_3_fun.7 = (bf16[640,2560]{1,0:T(8,128)(2,1)}, bf16[640,2560]{1,0:T(8,128)(2,1)}) custom-call(bf16[128,2560]{1,0:T(8,128)(2,1)S(1)} %collective-permute-done.18.far_ref, f32[640,2560]{1,0:T(8,128)S(1)} %copy-done.4, bf16[640,2560]{1,0:T(8,128)(2,1)S(1)} %get-tuple-element.94.mixed_ref, ...), custom_call_target="tpu_custom_call", output_to_operand_aliasing={{0}: (4, {}), {1}: (5, {})} | custom-call | flops 1966080 | bytes 3932160 | tf_op jit(solution)/shard_map/cond/branch_3_fun/pallas_call | solution.py:255
Async XLA Ops:
  1.5 77.8 %collective-permute-start.19 = (bf16[640,2560]{1,0:T(8,128)(2,1)}, bf16[640,2560]{1,0:T(8,128)(2,1)}, u32[]{:S(2)}, u32[]{:S(2)}) collective-permute-start(bf16[640,2560]{1,0:T(8,128)(2,1)} %bitcast.59), channel_id=1, source_target_pairs={{0,32},{4,36},{8,40},{12,44},{16,48},{20,52},{24,56},{28,60},{32,6... | collective-permute-start | bytes 9830408 | tf_op jit(solution)/shard_map/cond/branch_3_fun/ppermute | solution.py:272
  6.1 17.4 %all-to-all-start.1 = ((s32[4,1,256]{2,1,0:T(1,128)}), s32[4,1,256]{2,1,0:T(1,128)S(1)}, u32[]{:S(2)}, u32[]{:S(2)}) async-start(s32[4,1,256]{2,1,0:T(1,128)} %broadcast_in_dim.53), calls=%async_computation.1 | async-start | bytes 8192 | tf_op jit(solution)/shard_map/cond/branch_3_fun/all_to_all | solution.py:302
  17.0 118.4 %collective-permute-start.20 = (bf16[512,2560]{1,0:T(8,128)(2,1)}, bf16[512,2560]{1,0:T(8,128)(2,1)S(1)}, u32[]{:S(2)}, u32[]{:S(2)}) collective-permute-start(bf16[512,2560]{1,0:T(8,128)(2,1)} %slice_bitcast_fusion.7), channel_id=1, source_target_pairs={{0,32},{4,36},{8,40},{12,44},{16,48},{20,52},{24,56},{28,60},{32,6... | collective-permute-start | bytes 7864328 | tf_op jit(solution)/shard_map/cond/branch_3_fun/ppermute | solution.py:272
  20.3 128.1 %collective-permute-start.18 = (bf16[128,2560]{1,0:T(8,128)(2,1)}, bf16[128,2560]{1,0:T(8,128)(2,1)S(1)}, u32[]{:S(2)}, u32[]{:S(2)}) collective-permute-start(bf16[128,2560]{1,0:T(8,128)(2,1)} %slice_bitcast_fusion.8), channel_id=1, source_target_pairs={{0,32},{4,36},{8,40},{12,44},{16,48},{20,52},{24,56},{28,60},{32,6... | collective-permute-start | bytes 1966088 | tf_op jit(solution)/shard_map/cond/branch_3_fun/ppermute | solution.py:272
  23.5 55.9 %copy-start.15 = (f32[1,640]{1,0:T(1,128)S(1)}, f32[1,640]{1,0:T(1,128)}, u32[]{:S(2)}) copy-start(f32[1,640]{1,0:T(1,128)} %get-tuple-element.92.second_ref) | copy-start | bytes 7684 | tf_op jit(solution)/shard_map/cond
  35.8 2.3 %copy-start.9 = (bf16[1024,2560]{1,0:T(8,128)(2,1)}, bf16[1024,2560]{1,0:T(8,128)(2,1)S(1)}, u32[]{:S(2)}) copy-start(bf16[1024,2560]{1,0:T(8,128)(2,1)S(1)} %get-tuple-element.90.feats_ref) | copy-start | bytes 15728644 | tf_op jit(solution)/shard_map/cond
  135.4 2.9 %copy-start.4 = (f32[640,2560]{1,0:T(8,128)S(1)}, f32[640,2560]{1,0:T(8,128)}, u32[]{:S(2)}) copy-start(f32[640,2560]{1,0:T(8,128)} %get-tuple-element.93.lead_ref) | copy-start | bytes 19660804 | tf_op jit(solution)/shard_map/cond
where the time goes:
time: 150 us
  waiting for transfers between devices  76.7 us (51%)
  Pallas kernels  44.7 us (30%)
  starting transfers between devices  15.3 us (10%)
  local copies, waits for them, and re-layouts  11.8 us (8%)
    ppermute x3, waiting for transfers between devices, turned(): lax.ppermute(value, axis, [(i, (i + by) % size) for i in range(size)])  76.7 us
    pallas_call x1, Pallas kernels, make_gradient(): pl.pallas_call(partial(gradient_kernel, order), grid=(groups,), out_shape...  26.3 us
    pallas_call x1, Pallas kernels, make_features(): pl.pallas_call(features_kernel, grid=(count,), out_shape=(jax.ShapeDtypeS...  12.3 us
    ppermute x3, starting transfers between devices, turned(): lax.ppermute(value, axis, [(i, (i + by) % size) for i in range(size)])  7.73 us
    all_to_all x1, starting transfers between devices, step_at(): lax.all_to_all(jnp.broadcast_to(token_codes, (groups, tok_rows)), 'fsdp',...  7.56 us
    pallas_call x2, Pallas kernels, update(): pl.pallas_call(partial(update_kernel, order), grid=(rows // block,), out_...  6.03 us
    slice x2, local copies, waits for them, and re-layouts, step_at(): mom_far.append(turned(mom_own[low:high], 'dp', distance))  5.38 us
    cond x6, local copies, waits for them, and re-layouts  5.15 us
  transfers between devices with their start and end apart: 4, of which 3 were waited for; matrix products, arithmetic and copies ran while one was open for 4% of the time, Pallas kernels for 29%

commit v1 on v0

--- a/solution.py
+++ b/solution.py
@@ -16,6 +16,9 @@
 EPSILON = 1e-08
 LANES = 128
 BAND = 16
+TURNS = 4
+TOKS = 32
+SPLIT = (0, 9, 19, 35, 40)
 
 
 def turn_pair(turns):
@@ -38,30 +41,39 @@
     return (jnp.where(cos_minus, -cos_size, cos_size), jnp.where(sin_minus, -sin_size, sin_size))
 
 
-def features_kernel(first_ref, codes_ref, feats_ref, change_ref, near_ref, far_ref, band_ref, block_ref):
+def features_kernel(first_ref, codes_ref, feats_ref, change_ref, code_ref, band_ref, block_ref):
     tokens, width_all = feats_ref.shape
     own_rows = change_ref.shape[0]
     root = math.sqrt(2.0)
     row = jnp.broadcast_to(codes_ref[...], (LANES, tokens))
 
-    code = row.T
-    step = (2 * code + 977) & 65535
-    lane = lax.broadcasted_iota(jnp.int32, (tokens, LANES), 1)
-    near_ref[0], near_ref[1] = turn_pair((step * lane) & 65535)
-    far_cos, far_sin = turn_pair((code + step * (lane * LANES)) & 65535)
-    far_ref[0], far_ref[1] = far_cos * root, far_sin * root
+    code_ref[...] = row.T
+    half = LANES // 2
+    lane = lax.broadcasted_iota(jnp.int32, (TOKS, LANES), 1)
+    size = jnp.where(lane < half, root, 1.0)
 
     def some_tokens(k, _):
-        rows = pl.ds(k * 32, 32)
-        near_cos, near_sin = near_ref[0, rows, :], near_ref[1, rows, :]
-        far_cos, far_sin = far_ref[0, rows, :], far_ref[1, rows, :]
-        for a in range(width_all // LANES):
-            feats_ref[rows, a * LANES : (a + 1) * LANES] = (
-                far_cos[:, a : a + 1] * near_cos - far_sin[:, a : a + 1] * near_sin
-            ).astype(feats_ref.dtype)
-        return 0
-
-    lax.fori_loop(0, tokens // 32, some_tokens, 0)
+        rows = pl.ds(pl.multiple_of(k * TOKS, TOKS), TOKS)
+        code = code_ref[rows, :]
+        step = (2 * code + 977) & 65535
+        near_cos, near_sin = turn_pair((step * lane) & 65535)
+        far_turns = jnp.where(lane < half, code + step * (lane * (TURNS * LANES)), step * ((lane - half) * LANES))
+        far_cos, far_sin = turn_pair(far_turns & 65535)
+        far_cos, far_sin = far_cos * size, far_sin * size
+        near = [(near_cos, near_sin)]
+        for q in range(half + 1, half + TURNS):
+            by_cos, by_sin = far_cos[:, q : q + 1], far_sin[:, q : q + 1]
+            near.append((near_cos * by_cos - near_sin * by_sin, near_sin * by_cos + near_cos * by_sin))
+        for p in range(width_all // (TURNS * LANES)):
+            by_cos, by_sin = far_cos[:, p : p + 1], far_sin[:, p : p + 1]
+            for q, (one_cos, one_sin) in enumerate(near):
+                low = (p * TURNS + q) * LANES
+                feats_ref[rows, low : low + LANES] = (by_cos * one_cos - by_sin * one_sin).astype(
+                    feats_ref.dtype
+                )
+        return 0
+
+    lax.fori_loop(0, tokens // TOKS, some_tokens, 0)
 
     blocks = own_rows // BAND
     band = lax.broadcasted_iota(jnp.int32, (BAND, tokens), 0)
@@ -106,21 +118,20 @@
             pl.BlockSpec((own_rows, tok_rows), lambda s: (0, s)),
         ),
         scratch_shapes=[
-            pltpu.VMEM((2, tok_rows, LANES), jnp.float32),
-            pltpu.VMEM((2, tok_rows, LANES), jnp.float32),
+            pltpu.VMEM((tok_rows, LANES), jnp.int32),
             pltpu.VMEM((4, BAND, tok_rows), jnp.float32),
             pltpu.VMEM((4, own_rows // BAND, tok_rows), jnp.float32),
         ],
-        compiler_params=pltpu.CompilerParams(vmem_limit_bytes=32 * 2**20),
+        compiler_params=pltpu.CompilerParams(vmem_limit_bytes=12 * 2**20),
         cost_estimate=pl.CostEstimate(
-            flops=12 * 10**9, bytes_accessed=8 * 2**20, transcendentals=0
+            flops=9 * 10**9, bytes_accessed=8 * 2**20, transcendentals=0
         ),
     )(first_col.reshape(1), codes[:, None, :])
 
 
-def gradient_kernel(order, own_ref, far_ref, feats_ref, change_ref, mom_ref, second_ref, mixed_ref, lead_ref, *refs):
+def gradient_kernel(order, tile, own_ref, far_ref, feats_ref, change_ref, mom_ref, second_ref, mixed_ref, lead_ref, *refs):
     new_ref, rate_ref = refs[:2][::order]
-    error_ref, column_ref = refs[2:]
+    hidden_ref, error_ref, column_ref = refs[2:]
     sequence = pl.program_id(0)
     own_rows, width_all = own_ref.shape
     tokens = feats_ref.shape[0]
@@ -137,29 +148,29 @@
 
         lax.fori_loop(0, own_rows // 16, mix, 0)
 
-    half = own_rows // 2
+    hidden_ref[...] = lax.dot_general(
+        mixed_ref[...], feats_ref[...], (((1,), (1,)), ((), ())), preferred_element_type=jnp.float32
+    )
+    keep = lax.broadcasted_iota(jnp.int32, (32, tokens), 1) < tokens - 1
 
     def forward(k, _):
-        rows = pl.ds(pl.multiple_of(k * half, half), half)
-        hidden = lax.dot_general(
-            mixed_ref[rows, :], feats_ref[...], (((1,), (1,)), ((), ())), preferred_element_type=jnp.float32
-        )
+        rows = pl.ds(pl.multiple_of(k * 32, 32), 32)
+        hidden = hidden_ref[rows, :]
         squared = hidden * hidden
         tangent = jnp.tanh(GELU_SCALE * hidden * (1.0 + GELU_CUBIC * squared))
         value = 0.5 * hidden * (1.0 + tangent)
         slope = 0.5 * (1.0 + tangent) + 0.5 * hidden * (1.0 - tangent * tangent) * GELU_SCALE * (
             1.0 + 3.0 * GELU_CUBIC * squared
         )
-        keep = lax.broadcasted_iota(jnp.int32, (half, tokens), 1) < tokens - 1
         error_ref[rows, :] = jnp.where(keep, (change_ref[rows, :] + value) * slope, 0.0).astype(
             error_ref.dtype
         )
         return 0
 
-    lax.fori_loop(0, 2, forward, 0)
+    lax.fori_loop(0, own_rows // 32, forward, 0)
 
     def backward(k, _):
-        cut = pl.ds(pl.multiple_of(k * 256, 256), 256)
+        cut = pl.ds(pl.multiple_of(k * tile, tile), tile)
         term = lax.dot_general(
             error_ref[...], feats_ref[:, cut], (((1,), (0,)), ((), ())), preferred_element_type=jnp.float32
         )
@@ -167,7 +178,7 @@
         lead_ref[:, cut] = lead_ref[:, cut] + term
         return 0
 
-    lax.fori_loop(0, width_all // 256, backward, 0)
+    lax.fori_loop(0, width_all // tile, backward, 0)
 
     @pl.when(sequence == pl.num_programs(0) - 1)
     def _():
@@ -191,7 +202,7 @@
         rate_ref[...] = jnp.broadcast_to(rate, (LANES, own_rows)).T[:, :1]
 
 
-def make_gradient(own, far, feats, change, mom_own, second, tok_rows, order):
+def make_gradient(own, far, feats, change, mom_own, second, tok_rows, order, tile):
     own_rows, width_all = own.shape
     groups = feats.shape[0] // tok_rows
 
@@ -202,7 +213,7 @@
         return pl.BlockSpec(shape, lambda s: (0, 0), pipeline_mode=pl.Buffered(1))
 
     return pl.pallas_call(
-        partial(gradient_kernel, order),
+        partial(gradient_kernel, order, tile),
         grid=(groups,),
         out_shape=tuple(jax.ShapeDtypeStruct(s, t) for s, t in zip(shapes, types)),
         in_specs=[
@@ -215,10 +226,11 @@
         ],
         out_specs=tuple(whole(s) for s in shapes),
         scratch_shapes=[
+            pltpu.VMEM((own_rows, tok_rows), jnp.float32),
             pltpu.VMEM((own_rows, tok_rows), jnp.bfloat16),
             pltpu.VMEM((own_rows, LANES), jnp.float32),
         ],
-        compiler_params=pltpu.CompilerParams(vmem_limit_bytes=48 * 2**20),
+        compiler_params=pltpu.CompilerParams(vmem_limit_bytes=30 * 2**20),
         cost_estimate=pl.CostEstimate(
             flops=30 * 10**9,
             bytes_accessed=30 * 2**20,
@@ -244,11 +256,10 @@
 
 def update(first, far, lead, mixed, rate, before, order):
     rows, width_all = far.shape
-    block = max(b for b in range(16, 161, 16) if rows % b == 0 and first % b == 0)
-    skip = first // block
-
-    def cut(width, skip=skip):
-        return pl.BlockSpec((block, width), lambda i: (skip + i, 0))
+    block = max(b for b in range(16, 97, 16) if rows % b == 0)
+
+    def piece(width):
+        return pl.BlockSpec((pl.Element(block), pl.Element(width)), lambda i: ((first // 16 + i * (block // 16)) * 16, 0))
 
     whole = jax.ShapeDtypeStruct(lead.shape, jnp.bfloat16)
     held = () if before is None else tuple(before)
@@ -256,11 +267,11 @@
         partial(update_kernel, order),
         grid=(rows // block,),
         out_shape=(whole, whole),
-        in_specs=[cut(width_all, 0), cut(width_all), cut(width_all), cut(1)]
+        in_specs=[pl.BlockSpec((block, width_all), lambda i: (i, 0)), piece(width_all), piece(width_all), piece(1)]
         + [pl.BlockSpec(memory_space=pl.ANY)] * len(held),
-        out_specs=(cut(width_all), cut(width_all)),
+        out_specs=(piece(width_all), piece(width_all)),
         input_output_aliases={4 + k: k for k in range(len(held))},
-        compiler_params=pltpu.CompilerParams(vmem_limit_bytes=32 * 2**20),
+        compiler_params=pltpu.CompilerParams(vmem_limit_bytes=20 * 2**20),
         cost_estimate=pl.CostEstimate(
             flops=6 * rows * width_all, bytes_accessed=12 * rows * width_all, transcendentals=0
         ),
@@ -270,6 +281,10 @@
 def turned(value, axis, by):
     size = lax.axis_size(axis)
     return lax.ppermute(value, axis, [(i, (i + by) % size) for i in range(size)])
+
+
+def after(value, *others):
+    return lax.optimization_barrier((value, *others))[0]
 
 
 def long_way(distance, size):
@@ -294,38 +309,48 @@
     weights, mom_own = params[0], moments[0]
 
     weights_far = turned(weights, "dp", distance)
+    relay = distance in (4, 16)
+    if relay:
+        starts = tuple(own_rows * k // 40 for k in SPLIT)
+    elif distance == 1:
+        starts = tuple(own_rows * k // 10 for k in (0, 8, 10))
+    else:
+        starts = tuple(own_rows * k // 10 for k in (0, 9, 10))
+    mom_own_parts = []
+    for low, high in zip(starts, starts[1:]):
+        whole = after(mom_own, mom_own_parts[-1]) if relay and len(mom_own_parts) >= 2 else mom_own
+        mom_own_parts.append(whole[low:high])
     if distance <= 2:
         codes = jnp.concatenate(
             [token_codes] + [turned(token_codes, "fsdp", k) for k in range(1, groups)]
         )
     else:
+        own_codes = after(token_codes, mom_own_parts[2]) if relay else token_codes
         codes = lax.all_to_all(
-            jnp.broadcast_to(token_codes, (groups, tok_rows)), "fsdp", 0, 0, tiled=True
+            jnp.broadcast_to(own_codes, (groups, tok_rows)), "fsdp", 0, 0, tiled=True
         )
     first_col = lax.axis_index("fsdp") * own_rows
-    relay = distance in (4, 16)
-    if relay:
-        starts = (0, own_rows * 9 // 20, own_rows * 3 // 4, own_rows)
-    else:
-        starts = (0, own_rows * 4 // 5, own_rows)
     mom_far = []
     feats, change = make_features(codes, first_col, tok_rows, own_rows, width_all)
     if relay:
         first, second_hop, last = long_way(distance, lax.axis_size("dp"))
-        relayed = lax.ppermute(mom_own[: starts[1]], "dp", first)
-        relayed = lax.ppermute(relayed, "dp", second_hop)
-        relayed, feats, change = lax.optimization_barrier((relayed, feats, change))
-        mom_far.append(lax.ppermute(relayed, "dp", last))
-    done = len(mom_far)
-    for low, high in zip(starts[done:], starts[done + 1 :]):
-        mom_far.append(turned(mom_own[low:high], "dp", distance))
+        one, two = (lax.ppermute(part, "dp", first) for part in mom_own_parts[:2])
+        one_next = lax.ppermute(one, "dp", second_hop)
+        two_next = lax.ppermute(after(two, one), "dp", second_hop)
+        mom_far.append(lax.ppermute(one_next, "dp", last))
+        mom_far.append(lax.ppermute(after(two_next, one_next, feats, change), "dp", last))
+    for part in mom_own_parts[len(mom_far) :]:
+        mom_far.append(turned(part, "dp", distance))
 
     mixed, lead, *columns = make_gradient(
-        weights, weights_far, feats, change, mom_own, second, tok_rows, order
+        weights, weights_far, feats, change, mom_own, second, tok_rows, order, width_all // 2 if distance == 1 else 256
     )
     second_new, rate = columns[::order]
     outs = None
-    for low, far in zip(starts, mom_far):
+    pieces = list(zip(starts, mom_far))
+    if relay:
+        pieces[1], pieces[2] = pieces[2], pieces[1]
+    for low, far in pieces:
         outs = update(low, far, lead, mixed, rate, outs, order)
     param_new, mom_new = outs[::order]
     return (param_new[None], mom_new[None], second_new)

time: 150 us -> 116 us (0.77)
  waiting for transfers between devices: 76.7 us -> 43.9 us
  starting transfers between devices: 15.3 us -> 25 us
  Pallas kernels: 44.7 us -> 38.4 us
  local copies, waits for them, and re-layouts: 11.8 us -> 7.15 us
    ppermute x3, waiting for transfers between devices: 76.7 us -> 2.31 us  [turned(): lax.ppermute(value, axis, [(i, (i + by) % size) for i in range(size)])]
    ppermute x0 -> x6, waiting for transfers between devices: none -> 41.6 us  [the longest x2 18.6 us: step_at(): one, two = (lax.ppermute(part, 'dp', first) for part in mom_own_parts[:2])]
    ppermute x0 -> x6, starting transfers between devices: none -> 14.6 us  [the longest x1 3.69 us: step_at(): one_next = lax.ppermute(one, 'dp', second_hop)]
    cond x6 -> x8, local copies, waits for them, and re-layouts: 5.15 us -> 0.02 us
    ppermute x3, starting transfers between devices: 7.73 us -> 2.89 us  [turned(): lax.ppermute(value, axis, [(i, (i + by) % size) for i in range(size)])]
    pallas_call x1, Pallas kernels: 12.3 us -> 8.05 us  [make_features(): pl.pallas_call(features_kernel, grid=(count,), out_shape=(jax.ShapeDtypeS...]
    pallas_call x1, Pallas kernels: 26.3 us -> 22.4 us  [make_gradient(): pl.pallas_call(partial(gradient_kernel, order, tile), grid=(groups,), out...]
    pallas_call x2 -> x4, Pallas kernels: 6.03 us -> 7.98 us  [update(): pl.pallas_call(partial(update_kernel, order), grid=(rows // block,), out_...]
  transfers between devices with their start and end apart: 4 -> 10, of which waited for: 3 -> 4; matrix products, arithmetic and copies ran while one was open for 4% -> 6% of each run, Pallas kernels for 29% -> 32%
where the time goes in v1:
time: 116 us
  waiting for transfers between devices  43.9 us (38%)
  Pallas kernels  38.4 us (33%)
  starting transfers between devices  25 us (22%)
  local copies, waits for them, and re-layouts  7.15 us (6%)
  between operations  1.29 us (1%)
    pallas_call x1, Pallas kernels, make_gradient(): pl.pallas_call(partial(gradient_kernel, order, tile), grid=(groups,), out...  22.4 us
    ppermute x2, waiting for transfers between devices, step_at(): one, two = (lax.ppermute(part, 'dp', first) for part in mom_own_parts[:2])  18.6 us
    ppermute x1, waiting for transfers between devices, step_at(): two_next = lax.ppermute(after(two, one), 'dp', second_hop)  13.9 us
    ppermute x1, waiting for transfers between devices, step_at(): one_next = lax.ppermute(one, 'dp', second_hop)  9.15 us
    pallas_call x1, Pallas kernels, make_features(): pl.pallas_call(features_kernel, grid=(count,), out_shape=(jax.ShapeDtypeS...  8.05 us
    pallas_call x4, Pallas kernels, update(): pl.pallas_call(partial(update_kernel, order), grid=(rows // block,), out_...  7.98 us
    all_to_all x1, starting transfers between devices, step_at(): lax.all_to_all(jnp.broadcast_to(own_codes, (groups, tok_rows)), 'fsdp', 0...  7.56 us
    slice x4, local copies, waits for them, and re-layouts, step_at(): mom_own_parts.append(whole[low:high])  6.54 us
  transfers between devices with their start and end apart: 10, of which 4 were waited for; matrix products, arithmetic and copies ran while one was open for 6% of the time, Pallas kernels for 32%

profile of v1, /device:TPU:32, one launch (start us, length us, event | category | flops | bytes accessed | tf_op | source)
XLA Modules:
  0.0 116.1 jit_solution(3464697531292395913)
XLA Ops:
  1.3 114.8 %conditional.1 = (f32[1,640]{1,0:T(1,128)}, bf16[640,2560]{1,0:T(8,128)(2,1)}, bf16[640,2560]{1,0:T(8,128)(2,1)}) conditional(s32[]{:T(128)} %clamp.3, (bf16[1,640,2560]{2,1,0:T(8,128)(2,1)}, bf16[1,640,2560]{2,1,0:T(8,128)(2,1)}, s32[1,256]{1,0:T(1,128)}, f32[1,640]{1,0:T(1,128)}) %tuple.37, ...), branch_computations={%region_0.1_spmd, %region_1.2_spmd, %region_2.3_spmd, %region_3.4_... | conditional | flops 39009832960 | bytes 130973232 | solution.py:362
  1.5 0.0 copy-start.7
  1.5 1.7 %collective-permute-start.13 = (bf16[640,2560]{1,0:T(8,128)(2,1)}, bf16[640,2560]{1,0:T(8,128)(2,1)}, u32[]{:S(2)}, u32[]{:S(2)}) collective-permute-start(bf16[640,2560]{1,0:T(8,128)(2,1)} %bitcast.57), channel_id=1, source_target_pairs={{0,16},{4,20},{8,24},{12,28},{16,32},{20,36},{24,40},{28,44},{32,4... | collective-permute-start | bytes 9830408 | tf_op jit(solution)/shard_map/cond/branch_2_fun/ppermute | solution.py:283
  3.2 2.1 %slice_bitcast_fusion.4 = bf16[160,2560]{1,0:T(8,128)(2,1)} fusion(bf16[1,640,2560]{2,1,0:T(8,128)(2,1)} %get-tuple-element.68), kind=kLoop, calls=%fused_computation.6 | loop fusion | bytes 1638400 | tf_op jit(solution)/shard_map/cond/branch_2_fun/slice | solution.py:322
  5.3 2.6 %collective-permute-start.14 = (bf16[160,2560]{1,0:T(8,128)(2,1)}, bf16[160,2560]{1,0:T(8,128)(2,1)}, u32[]{:S(2)}, u32[]{:S(2)}) collective-permute-start(bf16[160,2560]{1,0:T(8,128)(2,1)} %slice_bitcast_fusion.4), channel_id=1, source_target_pairs={{0,48},{4,52},{8,56},{12,60},{16,0},{20,4},{24,8},{28,12},{32,16},... | collective-permute-start | bytes 2457608 | tf_op jit(solution)/shard_map/cond/branch_2_fun/ppermute | solution.py:337
  7.8 2.0 %slice_bitcast_fusion.5 = bf16[144,2560]{1,0:T(8,128)(2,1)} fusion(bf16[1,640,2560]{2,1,0:T(8,128)(2,1)} %get-tuple-element.68), kind=kLoop, calls=%fused_computation.7 | loop fusion | bytes 1474560 | tf_op jit(solution)/shard_map/cond/branch_2_fun/slice | solution.py:322
  9.9 0.9 collective-permute-start.15
  10.7 1.4 %slice.58 = bf16[256,2560]{1,0:T(8,128)(2,1)S(1)} slice(bf16[640,2560]{1,0:T(8,128)(2,1)} %bitcast.43), slice={[304:560], [0:2560]} | slice | bytes 2621440 | tf_op jit(solution)/shard_map/cond/branch_2_fun/slice | solution.py:322
  12.1 0.0 copy-done.7
  12.2 0.6 broadcast_in_dim.40
  12.8 7.6 %all-to-all-start = ((s32[4,1,256]{2,1,0:T(1,128)}), s32[4,1,256]{2,1,0:T(1,128)S(1)}, u32[]{:S(2)}, u32[]{:S(2)}) async-start(s32[4,1,256]{2,1,0:T(1,128)} %broadcast_in_dim.40), calls=%async_computation | async-start | bytes 8192 | tf_op jit(solution)/shard_map/cond/branch_2_fun/all_to_all | solution.py:329
  20.3 1.1 collective-permute-start.19
  21.5 1.0 slice.59
  22.5 0.1 collective-permute-start.12
  22.6 18.6 %collective-permute-done.15 = bf16[144,2560]{1,0:T(8,128)(2,1)} collective-permute-done((bf16[144,2560]{1,0:T(8,128)(2,1)}, bf16[144,2560]{1,0:T(8,128)(2,1)}, u32[]{:S(2)}, u32[]{:S(2)}) %collective-permute-start.15) | collective-permute-done | bytes 737312 | tf_op jit(solution)/shard_map/cond/branch_2_fun/ppermute | solution.py:337
  41.2 3.7 %collective-permute-start.17 = (bf16[144,2560]{1,0:T(8,128)(2,1)}, bf16[144,2560]{1,0:T(8,128)(2,1)}, u32[]{:S(2)}, u32[]{:S(2)}) collective-permute-start(bf16[144,2560]{1,0:T(8,128)(2,1)} %collective-permute-done.15), channel_id=1, source_target_pairs={{0,48},{4,52},{8,56},{12,60},{16,0},{20,4},{24,8},{28,12},{32,80},... | collective-permute-start | bytes 2211848 | tf_op jit(solution)/shard_map/cond/branch_2_fun/ppermute | solution.py:338
  44.9 0.0 collective-permute-done.14
  44.9 0.0 collective-permute-start.16
  44.9 0.0 all-to-all-done.codes_ref
  44.9 0.0 copy-start.2
  44.9 0.0 copy-start.11
  44.9 0.0 copy-start.16
  44.9 8.0 %branch_2_fun.6 = (bf16[1024,2560]{1,0:T(8,128)(2,1)S(1)}, f32[640,1024]{1,0:T(8,128)S(1)}) custom-call(s32[1]{0:T(128)} %bitcast.11.first_ref, s32[4,1,256]{2,1,0:T(1,128)S(1)} %all-to-all-done.codes_ref), custom_call_target="tpu_custom_call" | custom-call | flops 8999999488 | bytes 8388608 | tf_op jit(solution)/shard_map/cond/branch_2_fun/pallas_call | solution.py:105
  53.0 9.2 %collective-permute-done.17 = bf16[144,2560]{1,0:T(8,128)(2,1)} collective-permute-done((bf16[144,2560]{1,0:T(8,128)(2,1)}, bf16[144,2560]{1,0:T(8,128)(2,1)}, u32[]{:S(2)}, u32[]{:S(2)}) %collective-permute-start.17) | collective-permute-done | bytes 737312 | tf_op jit(solution)/shard_map/cond/branch_2_fun/ppermute | solution.py:338
  62.1 3.7 %collective-permute-start.20 = (bf16[144,2560]{1,0:T(8,128)(2,1)}, bf16[144,2560]{1,0:T(8,128)(2,1)S(1)}, u32[]{:S(2)}, u32[]{:S(2)}) collective-permute-start(bf16[144,2560]{1,0:T(8,128)(2,1)} %collective-permute-done.17), channel_id=1, source_target_pairs={{0,48},{4,52},{8,56},{12,60},{16,0},{20,4},{24,8},{28,12},{32,16},... | collective-permute-start | bytes 2211848 | tf_op jit(solution)/shard_map/cond/branch_2_fun/ppermute | solution.py:340
  65.8 13.9 %collective-permute-done.16 = bf16[160,2560]{1,0:T(8,128)(2,1)} collective-permute-done((bf16[160,2560]{1,0:T(8,128)(2,1)}, bf16[160,2560]{1,0:T(8,128)(2,1)}, u32[]{:S(2)}, u32[]{:S(2)}) %collective-permute-start.16) | collective-permute-done | bytes 819232 | tf_op jit(solution)/shard_map/cond/branch_2_fun/ppermute | solution.py:339
  79.7 3.7 %collective-permute-start.18 = (bf16[160,2560]{1,0:T(8,128)(2,1)}, bf16[160,2560]{1,0:T(8,128)(2,1)S(1)}, u32[]{:S(2)}, u32[]{:S(2)}) collective-permute-start(bf16[160,2560]{1,0:T(8,128)(2,1)} %collective-permute-done.16), channel_id=1, source_target_pairs={{0,48},{4,52},{8,56},{12,60},{16,0},{20,4},{24,8},{28,12},{32,16},... | collective-permute-start | bytes 2457608 | tf_op jit(solution)/shard_map/cond/branch_2_fun/ppermute | solution.py:341
  83.4 0.0 collective-permute-done.13.far_ref
  83.4 0.0 copy-done.2
  83.4 0.0 copy-done.11
  83.4 0.0 copy-done.16
  83.4 22.4 %branch_2_fun.7 = (bf16[640,2560]{1,0:T(8,128)(2,1)S(1)}, f32[640,2560]{1,0:T(8,128)S(1)}, f32[1,640]{1,0:T(1,128)}, f32[640,1]{1,0:T(8,128)S(1)}) custom-call(bf16[640,2560]{1,0:T(8,128)(2,1)S(1)} %bitcast.58, bf16[640,2560]{1,0:T(8,128)(2,1)} %collective-permute-done.13.far_ref, bf16[1024,2560]{1,0:T(8,128)(2,1)S(1)} %get-tuple-element.74.feats_ref, ...), custom_call_target="tpu_custom_call" | custom-call | flops 30000001024 | bytes 31457280 | tf_op jit(solution)/shard_map/cond/branch_2_fun/pallas_call | solution.py:215
  105.7 0.0 collective-permute-done.20.far_ref
  105.8 2.1 %branch_2_fun.8 = (bf16[640,2560]{1,0:T(8,128)(2,1)}, bf16[640,2560]{1,0:T(8,128)(2,1)}) custom-call(bf16[144,2560]{1,0:T(8,128)(2,1)S(1)} %collective-permute-done.20.far_ref, f32[640,2560]{1,0:T(8,128)S(1)} %get-tuple-element.77.lead_ref, bf16[640,2560]{1,0:T(8,128)(2,1)S(1)} %get-tuple-element.78.mixed_ref, f32[640,1]{1,0:T(8,128)S(1)} %get-tuple-element.79.rate_ref), custom_call_target="tpu_custom_call" | custom-call | flops 2211840 | bytes 4423680 | tf_op jit(solution)/shard_map/cond/branch_2_fun/pallas_call | solution.py:266
  107.8 0.0 collective-permute-done.19.far_ref
  107.9 2.8 %branch_2_fun.9 = (bf16[640,2560]{1,0:T(8,128)(2,1)}, bf16[640,2560]{1,0:T(8,128)(2,1)}) custom-call(bf16[256,2560]{1,0:T(8,128)(2,1)S(1)} %collective-permute-done.19.far_ref, f32[640,2560]{1,0:T(8,128)S(1)} %get-tuple-element.77.lead_ref, bf16[640,2560]{1,0:T(8,128)(2,1)S(1)} %get-tuple-element.78.mixed_ref, ...), custom_call_target="tpu_custom_call", output_to_operand_aliasing={{0}: (4, {}), {1}: (5, {})} | custom-call | flops 3932160 | bytes 7864320 | tf_op jit(solution)/shard_map/cond/branch_2_fun/pallas_call | solution.py:266
  110.6 0.0 collective-permute-done.18.far_ref
  110.7 1.8 %branch_2_fun.10 = (bf16[640,2560]{1,0:T(8,128)(2,1)}, bf16[640,2560]{1,0:T(8,128)(2,1)}) custom-call(bf16[160,2560]{1,0:T(8,128)(2,1)S(1)} %collective-permute-done.18.far_ref, f32[640,2560]{1,0:T(8,128)S(1)} %get-tuple-element.77.lead_ref, bf16[640,2560]{1,0:T(8,128)(2,1)S(1)} %get-tuple-element.78.mixed_ref, ...), custom_call_target="tpu_custom_call", output_to_operand_aliasing={{0}: (4, {}), {1}: (5, {})} | custom-call | flops 2457600 | bytes 4915200 | tf_op jit(solution)/shard_map/cond/branch_2_fun/pallas_call | solution.py:266
  112.5 2.3 %collective-permute-done.12.far_ref = bf16[80,2560]{1,0:T(8,128)(2,1)S(1)} collective-permute-done((bf16[80,2560]{1,0:T(8,128)(2,1)S(1)}, bf16[80,2560]{1,0:T(8,128)(2,1)S(1)}, u32[]{:S(2)}, u32[]{:S(2)}) %collective-permute-start.12) | collective-permute-done | bytes 409632 | tf_op jit(solution)/shard_map/cond/branch_2_fun/ppermute | solution.py:283
  114.8 1.3 %branch_2_fun.11 = (bf16[640,2560]{1,0:T(8,128)(2,1)}, bf16[640,2560]{1,0:T(8,128)(2,1)}) custom-call(bf16[80,2560]{1,0:T(8,128)(2,1)S(1)} %collective-permute-done.12.far_ref, f32[640,2560]{1,0:T(8,128)S(1)} %get-tuple-element.77.lead_ref, bf16[640,2560]{1,0:T(8,128)(2,1)S(1)} %get-tuple-element.78.mixed_ref, ...), custom_call_target="tpu_custom_call", output_to_operand_aliasing={{0}: (4, {}), {1}: (5, {})} | custom-call | flops 1228800 | bytes 2457600 | tf_op jit(solution)/shard_map/cond/branch_2_fun/pallas_call | solution.py:266
Async XLA Ops:
  1.5 10.6 %copy-start.7 = (s32[1,256]{1,0:T(1,128)S(1)}, s32[1,256]{1,0:T(1,128)}, u32[]{:S(2)}) copy-start(s32[1,256]{1,0:T(1,128)} %get-tuple-element.73) | copy-start | bytes 3076 | tf_op jit(solution)/shard_map/cond
  1.5 81.9 %collective-permute-start.13 = (bf16[640,2560]{1,0:T(8,128)(2,1)}, bf16[640,2560]{1,0:T(8,128)(2,1)}, u32[]{:S(2)}, u32[]{:S(2)}) collective-permute-start(bf16[640,2560]{1,0:T(8,128)(2,1)} %bitcast.57), channel_id=1, source_target_pairs={{0,16},{4,20},{8,24},{12,28},{16,32},{20,36},{24,40},{28,44},{32,4... | collective-permute-start | bytes 9830408 | tf_op jit(solution)/shard_map/cond/branch_2_fun/ppermute | solution.py:283
  5.3 39.6 %collective-permute-start.14 = (bf16[160,2560]{1,0:T(8,128)(2,1)}, bf16[160,2560]{1,0:T(8,128)(2,1)}, u32[]{:S(2)}, u32[]{:S(2)}) collective-permute-start(bf16[160,2560]{1,0:T(8,128)(2,1)} %slice_bitcast_fusion.4), channel_id=1, source_target_pairs={{0,48},{4,52},{8,56},{12,60},{16,0},{20,4},{24,8},{28,12},{32,16},... | collective-permute-start | bytes 2457608 | tf_op jit(solution)/shard_map/cond/branch_2_fun/ppermute | solution.py:337
  9.9 31.3 %collective-permute-start.15 = (bf16[144,2560]{1,0:T(8,128)(2,1)}, bf16[144,2560]{1,0:T(8,128)(2,1)}, u32[]{:S(2)}, u32[]{:S(2)}) collective-permute-start(bf16[144,2560]{1,0:T(8,128)(2,1)} %slice_bitcast_fusion.5), channel_id=1, source_target_pairs={{0,48},{4,52},{8,56},{12,60},{16,0},{20,4},{24,8},{28,12},{32,16},... | collective-permute-start | bytes 2211848 | tf_op jit(solution)/shard_map/cond/branch_2_fun/ppermute | solution.py:337
  12.8 32.2 %all-to-all-start = ((s32[4,1,256]{2,1,0:T(1,128)}), s32[4,1,256]{2,1,0:T(1,128)S(1)}, u32[]{:S(2)}, u32[]{:S(2)}) async-start(s32[4,1,256]{2,1,0:T(1,128)} %broadcast_in_dim.40), calls=%async_computation | async-start | bytes 8192 | tf_op jit(solution)/shard_map/cond/branch_2_fun/all_to_all | solution.py:329
  20.3 87.5 %collective-permute-start.19 = (bf16[256,2560]{1,0:T(8,128)(2,1)S(1)}, bf16[256,2560]{1,0:T(8,128)(2,1)S(1)}, u32[]{:S(2)}, u32[]{:S(2)}) collective-permute-start(bf16[256,2560]{1,0:T(8,128)(2,1)S(1)} %slice.58), channel_id=1, source_target_pairs={{0,16},{4,20},{8,24},{12,28},{16,32},{20,36},{24,40},{28,44},{32,4... | collective-permute-start | bytes 3932168 | tf_op jit(solution)/shard_map/cond/branch_2_fun/ppermute | solution.py:283
  22.5 92.3 %collective-permute-start.12 = (bf16[80,2560]{1,0:T(8,128)(2,1)S(1)}, bf16[80,2560]{1,0:T(8,128)(2,1)S(1)}, u32[]{:S(2)}, u32[]{:S(2)}) collective-permute-start(bf16[80,2560]{1,0:T(8,128)(2,1)S(1)} %slice.59), channel_id=1, source_target_pairs={{0,16},{4,20},{8,24},{12,28},{16,32},{20,36},{24,40},{28,44},{32,4... | collective-permute-start | bytes 1228808 | tf_op jit(solution)/shard_map/cond/branch_2_fun/ppermute | solution.py:283
  41.2 21.0 %collective-permute-start.17 = (bf16[144,2560]{1,0:T(8,128)(2,1)}, bf16[144,2560]{1,0:T(8,128)(2,1)}, u32[]{:S(2)}, u32[]{:S(2)}) collective-permute-start(bf16[144,2560]{1,0:T(8,128)(2,1)} %collective-permute-done.15), channel_id=1, source_target_pairs={{0,48},{4,52},{8,56},{12,60},{16,0},{20,4},{24,8},{28,12},{32,80},... | collective-permute-start | bytes 2211848 | tf_op jit(solution)/shard_map/cond/branch_2_fun/ppermute | solution.py:338
  44.9 34.8 %collective-permute-start.16 = (bf16[160,2560]{1,0:T(8,128)(2,1)}, bf16[160,2560]{1,0:T(8,128)(2,1)}, u32[]{:S(2)}, u32[]{:S(2)}) collective-permute-start(bf16[160,2560]{1,0:T(8,128)(2,1)} %collective-permute-done.14), channel_id=1, source_target_pairs={{0,48},{4,52},{8,56},{12,60},{16,0},{20,4},{24,8},{28,12},{32,80},... | collective-permute-start | bytes 2457608 | tf_op jit(solution)/shard_map/cond/branch_2_fun/ppermute | solution.py:339
  44.9 38.5 %copy-start.2 = (bf16[1,640,2560]{2,1,0:T(8,128)(2,1)S(1)}, bf16[1,640,2560]{2,1,0:T(8,128)(2,1)}, u32[]{:S(2)}) copy-start(bf16[1,640,2560]{2,1,0:T(8,128)(2,1)} %get-tuple-element.68) | copy-start | bytes 9830404 | tf_op jit(solution)/shard_map/cond
  44.9 38.5 %copy-start.11 = (bf16[1,640,2560]{2,1,0:T(8,128)(2,1)S(1)}, bf16[1,640,2560]{2,1,0:T(8,128)(2,1)}, u32[]{:S(2)}) copy-start(bf16[1,640,2560]{2,1,0:T(8,128)(2,1)} %get-tuple-element.71) | copy-start | bytes 9830404 | tf_op jit(solution)/shard_map/cond
  44.9 38.5 %copy-start.16 = (f32[1,640]{1,0:T(1,128)S(1)}, f32[1,640]{1,0:T(1,128)}, u32[]{:S(2)}) copy-start(f32[1,640]{1,0:T(1,128)} %get-tuple-element.76.second_ref) | copy-start | bytes 7684 | tf_op jit(solution)/shard_map/cond
  62.1 43.6 %collective-permute-start.20 = (bf16[144,2560]{1,0:T(8,128)(2,1)}, bf16[144,2560]{1,0:T(8,128)(2,1)S(1)}, u32[]{:S(2)}, u32[]{:S(2)}) collective-permute-start(bf16[144,2560]{1,0:T(8,128)(2,1)} %collective-permute-done.17), channel_id=1, source_target_pairs={{0,48},{4,52},{8,56},{12,60},{16,0},{20,4},{24,8},{28,12},{32,16},... | collective-permute-start | bytes 2211848 | tf_op jit(solution)/shard_map/cond/branch_2_fun/ppermute | solution.py:340
  79.7 31.0 %collective-permute-start.18 = (bf16[160,2560]{1,0:T(8,128)(2,1)}, bf16[160,2560]{1,0:T(8,128)(2,1)S(1)}, u32[]{:S(2)}, u32[]{:S(2)}) collective-permute-start(bf16[160,2560]{1,0:T(8,128)(2,1)} %collective-permute-done.16), channel_id=1, source_target_pairs={{0,48},{4,52},{8,56},{12,60},{16,0},{20,4},{24,8},{28,12},{32,16},... | collective-permute-start | bytes 2457608 | tf_op jit(solution)/shard_map/cond/branch_2_fun/ppermute | solution.py:341

commit v2 on v1

--- a/solution.py
+++ b/solution.py
@@ -318,7 +318,7 @@
         starts = tuple(own_rows * k // 10 for k in (0, 9, 10))
     mom_own_parts = []
     for low, high in zip(starts, starts[1:]):
-        whole = after(mom_own, mom_own_parts[-1]) if relay and len(mom_own_parts) >= 2 else mom_own
+        whole = after(mom_own, mom_own_parts[-1]) if len(mom_own_parts) > relay else mom_own
         mom_own_parts.append(whole[low:high])
     if distance <= 2:
         codes = jnp.concatenate(

time: 116 us -> 115 us (level)
  no operation moved by 1% of the time
where the time goes in v2:
time: 115 us; the launch traced here: 116 us
  waiting for transfers between devices  43.9 us (38%)
  Pallas kernels  38.4 us (33%)
  starting transfers between devices  25 us (22%)
  local copies, waits for them, and re-layouts  7.15 us (6%)
  between operations  1.29 us (1%)
    pallas_call x1, Pallas kernels, make_gradient(): pl.pallas_call(partial(gradient_kernel, order, tile), grid=(groups,), out...  22.4 us
    ppermute x2, waiting for transfers between devices, step_at(): one, two = (lax.ppermute(part, 'dp', first) for part in mom_own_parts[:2])  18.6 us
    ppermute x1, waiting for transfers between devices, step_at(): two_next = lax.ppermute(after(two, one), 'dp', second_hop)  13.9 us
    ppermute x1, waiting for transfers between devices, step_at(): one_next = lax.ppermute(one, 'dp', second_hop)  9.15 us
    pallas_call x1, Pallas kernels, make_features(): pl.pallas_call(features_kernel, grid=(count,), out_shape=(jax.ShapeDtypeS...  8.05 us
    pallas_call x4, Pallas kernels, update(): pl.pallas_call(partial(update_kernel, order), grid=(rows // block,), out_...  7.98 us
    all_to_all x1, starting transfers between devices, step_at(): lax.all_to_all(jnp.broadcast_to(own_codes, (groups, tok_rows)), 'fsdp', 0...  7.56 us
    slice x4, local copies, waits for them, and re-layouts, step_at(): mom_own_parts.append(whole[low:high])  6.54 us
  transfers between devices with their start and end apart: 10, of which 4 were waited for; matrix products, arithmetic and copies ran while one was open for 6% of the time, Pallas kernels for 32%

profile of v2, /device:TPU:32, one launch (start us, length us, event | category | flops | bytes accessed | tf_op | source)
XLA Modules:
  0.0 116.1 jit_solution(7818922127329546333)
XLA Ops:
  1.3 114.8 %conditional.1 = (f32[1,640]{1,0:T(1,128)}, bf16[640,2560]{1,0:T(8,128)(2,1)}, bf16[640,2560]{1,0:T(8,128)(2,1)}) conditional(s32[]{:T(128)} %clamp.3, (bf16[1,640,2560]{2,1,0:T(8,128)(2,1)}, bf16[1,640,2560]{2,1,0:T(8,128)(2,1)}, s32[1,256]{1,0:T(1,128)}, f32[1,640]{1,0:T(1,128)}) %tuple.40, ...), branch_computations={%region_0.1_spmd, %region_1.2_spmd, %region_2.3_spmd, %region_3.4_... | conditional | flops 39009832960 | bytes 130973232 | solution.py:362
  1.5 0.0 copy-start.7
  1.5 1.7 %collective-permute-start.13 = (bf16[640,2560]{1,0:T(8,128)(2,1)}, bf16[640,2560]{1,0:T(8,128)(2,1)}, u32[]{:S(2)}, u32[]{:S(2)}) collective-permute-start(bf16[640,2560]{1,0:T(8,128)(2,1)} %bitcast.54), channel_id=1, source_target_pairs={{0,16},{4,20},{8,24},{12,28},{16,32},{20,36},{24,40},{28,44},{32,4... | collective-permute-start | bytes 9830408 | tf_op jit(solution)/shard_map/cond/branch_2_fun/ppermute | solution.py:283
  3.2 2.1 %slice_bitcast_fusion.2 = bf16[160,2560]{1,0:T(8,128)(2,1)} fusion(bf16[1,640,2560]{2,1,0:T(8,128)(2,1)} %get-tuple-element.70), kind=kLoop, calls=%fused_computation.4 | loop fusion | bytes 1638400 | tf_op jit(solution)/shard_map/cond/branch_2_fun/slice | solution.py:322
  5.3 2.6 %collective-permute-start.14 = (bf16[160,2560]{1,0:T(8,128)(2,1)}, bf16[160,2560]{1,0:T(8,128)(2,1)}, u32[]{:S(2)}, u32[]{:S(2)}) collective-permute-start(bf16[160,2560]{1,0:T(8,128)(2,1)} %slice_bitcast_fusion.2), channel_id=1, source_target_pairs={{0,48},{4,52},{8,56},{12,60},{16,0},{20,4},{24,8},{28,12},{32,16},... | collective-permute-start | bytes 2457608 | tf_op jit(solution)/shard_map/cond/branch_2_fun/ppermute | solution.py:337
  7.8 2.0 %slice_bitcast_fusion.3 = bf16[144,2560]{1,0:T(8,128)(2,1)} fusion(bf16[1,640,2560]{2,1,0:T(8,128)(2,1)} %get-tuple-element.70), kind=kLoop, calls=%fused_computation.5 | loop fusion | bytes 1474560 | tf_op jit(solution)/shard_map/cond/branch_2_fun/slice | solution.py:322
  9.9 0.9 collective-permute-start.15
  10.7 1.4 %slice.50 = bf16[256,2560]{1,0:T(8,128)(2,1)S(1)} slice(bf16[640,2560]{1,0:T(8,128)(2,1)} %bitcast.39), slice={[304:560], [0:2560]} | slice | bytes 2621440 | tf_op jit(solution)/shard_map/cond/branch_2_fun/slice | solution.py:322
  12.1 0.0 copy-done.7
  12.2 0.6 broadcast_in_dim.40
  12.8 7.6 %all-to-all-start = ((s32[4,1,256]{2,1,0:T(1,128)}), s32[4,1,256]{2,1,0:T(1,128)S(1)}, u32[]{:S(2)}, u32[]{:S(2)}) async-start(s32[4,1,256]{2,1,0:T(1,128)} %broadcast_in_dim.40), calls=%async_computation | async-start | bytes 8192 | tf_op jit(solution)/shard_map/cond/branch_2_fun/all_to_all | solution.py:329
  20.3 1.1 collective-permute-start.19
  21.5 1.0 slice.51
  22.5 0.1 collective-permute-start.12
  22.6 18.6 %collective-permute-done.15 = bf16[144,2560]{1,0:T(8,128)(2,1)} collective-permute-done((bf16[144,2560]{1,0:T(8,128)(2,1)}, bf16[144,2560]{1,0:T(8,128)(2,1)}, u32[]{:S(2)}, u32[]{:S(2)}) %collective-permute-start.15) | collective-permute-done | bytes 737312 | tf_op jit(solution)/shard_map/cond/branch_2_fun/ppermute | solution.py:337
  41.2 3.7 %collective-permute-start.17 = (bf16[144,2560]{1,0:T(8,128)(2,1)}, bf16[144,2560]{1,0:T(8,128)(2,1)}, u32[]{:S(2)}, u32[]{:S(2)}) collective-permute-start(bf16[144,2560]{1,0:T(8,128)(2,1)} %collective-permute-done.15), channel_id=1, source_target_pairs={{0,48},{4,52},{8,56},{12,60},{16,0},{20,4},{24,8},{28,12},{32,80},... | collective-permute-start | bytes 2211848 | tf_op jit(solution)/shard_map/cond/branch_2_fun/ppermute | solution.py:338
  44.9 0.0 collective-permute-done.14
  44.9 0.0 collective-permute-start.16
  44.9 0.0 all-to-all-done.codes_ref
  44.9 0.0 copy-start.2
  44.9 0.0 copy-start.11
  44.9 0.0 copy-start.16
  44.9 8.0 %branch_2_fun.6 = (bf16[1024,2560]{1,0:T(8,128)(2,1)S(1)}, f32[640,1024]{1,0:T(8,128)S(1)}) custom-call(s32[1]{0:T(128)} %bitcast.9.first_ref, s32[4,1,256]{2,1,0:T(1,128)S(1)} %all-to-all-done.codes_ref), custom_call_target="tpu_custom_call" | custom-call | flops 8999999488 | bytes 8388608 | tf_op jit(solution)/shard_map/cond/branch_2_fun/pallas_call | solution.py:105
  53.0 9.2 %collective-permute-done.17 = bf16[144,2560]{1,0:T(8,128)(2,1)} collective-permute-done((bf16[144,2560]{1,0:T(8,128)(2,1)}, bf16[144,2560]{1,0:T(8,128)(2,1)}, u32[]{:S(2)}, u32[]{:S(2)}) %collective-permute-start.17) | collective-permute-done | bytes 737312 | tf_op jit(solution)/shard_map/cond/branch_2_fun/ppermute | solution.py:338
  62.1 3.7 %collective-permute-start.20 = (bf16[144,2560]{1,0:T(8,128)(2,1)}, bf16[144,2560]{1,0:T(8,128)(2,1)S(1)}, u32[]{:S(2)}, u32[]{:S(2)}) collective-permute-start(bf16[144,2560]{1,0:T(8,128)(2,1)} %collective-permute-done.17), channel_id=1, source_target_pairs={{0,48},{4,52},{8,56},{12,60},{16,0},{20,4},{24,8},{28,12},{32,16},... | collective-permute-start | bytes 2211848 | tf_op jit(solution)/shard_map/cond/branch_2_fun/ppermute | solution.py:340
  65.8 13.9 %collective-permute-done.16 = bf16[160,2560]{1,0:T(8,128)(2,1)} collective-permute-done((bf16[160,2560]{1,0:T(8,128)(2,1)}, bf16[160,2560]{1,0:T(8,128)(2,1)}, u32[]{:S(2)}, u32[]{:S(2)}) %collective-permute-start.16) | collective-permute-done | bytes 819232 | tf_op jit(solution)/shard_map/cond/branch_2_fun/ppermute | solution.py:339
  79.7 3.7 %collective-permute-start.18 = (bf16[160,2560]{1,0:T(8,128)(2,1)}, bf16[160,2560]{1,0:T(8,128)(2,1)S(1)}, u32[]{:S(2)}, u32[]{:S(2)}) collective-permute-start(bf16[160,2560]{1,0:T(8,128)(2,1)} %collective-permute-done.16), channel_id=1, source_target_pairs={{0,48},{4,52},{8,56},{12,60},{16,0},{20,4},{24,8},{28,12},{32,16},... | collective-permute-start | bytes 2457608 | tf_op jit(solution)/shard_map/cond/branch_2_fun/ppermute | solution.py:341
  83.4 0.0 collective-permute-done.13.far_ref
  83.4 0.0 copy-done.2
  83.4 0.0 copy-done.11
  83.4 0.0 copy-done.16
  83.4 22.4 %branch_2_fun.7 = (bf16[640,2560]{1,0:T(8,128)(2,1)S(1)}, f32[640,2560]{1,0:T(8,128)S(1)}, f32[1,640]{1,0:T(1,128)}, f32[640,1]{1,0:T(8,128)S(1)}) custom-call(bf16[640,2560]{1,0:T(8,128)(2,1)S(1)} %bitcast.55, bf16[640,2560]{1,0:T(8,128)(2,1)} %collective-permute-done.13.far_ref, bf16[1024,2560]{1,0:T(8,128)(2,1)S(1)} %get-tuple-element.76.feats_ref, ...), custom_call_target="tpu_custom_call" | custom-call | flops 30000001024 | bytes 31457280 | tf_op jit(solution)/shard_map/cond/branch_2_fun/pallas_call | solution.py:215
  105.7 0.0 collective-permute-done.20.far_ref
  105.8 2.1 %branch_2_fun.8 = (bf16[640,2560]{1,0:T(8,128)(2,1)}, bf16[640,2560]{1,0:T(8,128)(2,1)}) custom-call(bf16[144,2560]{1,0:T(8,128)(2,1)S(1)} %collective-permute-done.20.far_ref, f32[640,2560]{1,0:T(8,128)S(1)} %get-tuple-element.79.lead_ref, bf16[640,2560]{1,0:T(8,128)(2,1)S(1)} %get-tuple-element.80.mixed_ref, f32[640,1]{1,0:T(8,128)S(1)} %get-tuple-element.81.rate_ref), custom_call_target="tpu_custom_call" | custom-call | flops 2211840 | bytes 4423680 | tf_op jit(solution)/shard_map/cond/branch_2_fun/pallas_call | solution.py:266
  107.8 0.0 collective-permute-done.19.far_ref
  107.9 2.8 %branch_2_fun.9 = (bf16[640,2560]{1,0:T(8,128)(2,1)}, bf16[640,2560]{1,0:T(8,128)(2,1)}) custom-call(bf16[256,2560]{1,0:T(8,128)(2,1)S(1)} %collective-permute-done.19.far_ref, f32[640,2560]{1,0:T(8,128)S(1)} %get-tuple-element.79.lead_ref, bf16[640,2560]{1,0:T(8,128)(2,1)S(1)} %get-tuple-element.80.mixed_ref, ...), custom_call_target="tpu_custom_call", output_to_operand_aliasing={{0}: (4, {}), {1}: (5, {})} | custom-call | flops 3932160 | bytes 7864320 | tf_op jit(solution)/shard_map/cond/branch_2_fun/pallas_call | solution.py:266
  110.6 0.0 collective-permute-done.18.far_ref
  110.7 1.8 %branch_2_fun.10 = (bf16[640,2560]{1,0:T(8,128)(2,1)}, bf16[640,2560]{1,0:T(8,128)(2,1)}) custom-call(bf16[160,2560]{1,0:T(8,128)(2,1)S(1)} %collective-permute-done.18.far_ref, f32[640,2560]{1,0:T(8,128)S(1)} %get-tuple-element.79.lead_ref, bf16[640,2560]{1,0:T(8,128)(2,1)S(1)} %get-tuple-element.80.mixed_ref, ...), custom_call_target="tpu_custom_call", output_to_operand_aliasing={{0}: (4, {}), {1}: (5, {})} | custom-call | flops 2457600 | bytes 4915200 | tf_op jit(solution)/shard_map/cond/branch_2_fun/pallas_call | solution.py:266
  112.5 2.3 %collective-permute-done.12.far_ref = bf16[80,2560]{1,0:T(8,128)(2,1)S(1)} collective-permute-done((bf16[80,2560]{1,0:T(8,128)(2,1)S(1)}, bf16[80,2560]{1,0:T(8,128)(2,1)S(1)}, u32[]{:S(2)}, u32[]{:S(2)}) %collective-permute-start.12) | collective-permute-done | bytes 409632 | tf_op jit(solution)/shard_map/cond/branch_2_fun/ppermute | solution.py:283
  114.8 1.3 %branch_2_fun.11 = (bf16[640,2560]{1,0:T(8,128)(2,1)}, bf16[640,2560]{1,0:T(8,128)(2,1)}) custom-call(bf16[80,2560]{1,0:T(8,128)(2,1)S(1)} %collective-permute-done.12.far_ref, f32[640,2560]{1,0:T(8,128)S(1)} %get-tuple-element.79.lead_ref, bf16[640,2560]{1,0:T(8,128)(2,1)S(1)} %get-tuple-element.80.mixed_ref, ...), custom_call_target="tpu_custom_call", output_to_operand_aliasing={{0}: (4, {}), {1}: (5, {})} | custom-call | flops 1228800 | bytes 2457600 | tf_op jit(solution)/shard_map/cond/branch_2_fun/pallas_call | solution.py:266
Async XLA Ops:
  1.5 10.6 %copy-start.7 = (s32[1,256]{1,0:T(1,128)S(1)}, s32[1,256]{1,0:T(1,128)}, u32[]{:S(2)}) copy-start(s32[1,256]{1,0:T(1,128)} %get-tuple-element.75) | copy-start | bytes 3076 | tf_op jit(solution)/shard_map/cond
  1.5 81.9 %collective-permute-start.13 = (bf16[640,2560]{1,0:T(8,128)(2,1)}, bf16[640,2560]{1,0:T(8,128)(2,1)}, u32[]{:S(2)}, u32[]{:S(2)}) collective-permute-start(bf16[640,2560]{1,0:T(8,128)(2,1)} %bitcast.54), channel_id=1, source_target_pairs={{0,16},{4,20},{8,24},{12,28},{16,32},{20,36},{24,40},{28,44},{32,4... | collective-permute-start | bytes 9830408 | tf_op jit(solution)/shard_map/cond/branch_2_fun/ppermute | solution.py:283
  5.3 39.6 %collective-permute-start.14 = (bf16[160,2560]{1,0:T(8,128)(2,1)}, bf16[160,2560]{1,0:T(8,128)(2,1)}, u32[]{:S(2)}, u32[]{:S(2)}) collective-permute-start(bf16[160,2560]{1,0:T(8,128)(2,1)} %slice_bitcast_fusion.2), channel_id=1, source_target_pairs={{0,48},{4,52},{8,56},{12,60},{16,0},{20,4},{24,8},{28,12},{32,16},... | collective-permute-start | bytes 2457608 | tf_op jit(solution)/shard_map/cond/branch_2_fun/ppermute | solution.py:337
  9.9 31.3 %collective-permute-start.15 = (bf16[144,2560]{1,0:T(8,128)(2,1)}, bf16[144,2560]{1,0:T(8,128)(2,1)}, u32[]{:S(2)}, u32[]{:S(2)}) collective-permute-start(bf16[144,2560]{1,0:T(8,128)(2,1)} %slice_bitcast_fusion.3), channel_id=1, source_target_pairs={{0,48},{4,52},{8,56},{12,60},{16,0},{20,4},{24,8},{28,12},{32,16},... | collective-permute-start | bytes 2211848 | tf_op jit(solution)/shard_map/cond/branch_2_fun/ppermute | solution.py:337
  12.8 32.2 %all-to-all-start = ((s32[4,1,256]{2,1,0:T(1,128)}), s32[4,1,256]{2,1,0:T(1,128)S(1)}, u32[]{:S(2)}, u32[]{:S(2)}) async-start(s32[4,1,256]{2,1,0:T(1,128)} %broadcast_in_dim.40), calls=%async_computation | async-start | bytes 8192 | tf_op jit(solution)/shard_map/cond/branch_2_fun/all_to_all | solution.py:329
  20.3 87.5 %collective-permute-start.19 = (bf16[256,2560]{1,0:T(8,128)(2,1)S(1)}, bf16[256,2560]{1,0:T(8,128)(2,1)S(1)}, u32[]{:S(2)}, u32[]{:S(2)}) collective-permute-start(bf16[256,2560]{1,0:T(8,128)(2,1)S(1)} %slice.50), channel_id=1, source_target_pairs={{0,16},{4,20},{8,24},{12,28},{16,32},{20,36},{24,40},{28,44},{32,4... | collective-permute-start | bytes 3932168 | tf_op jit(solution)/shard_map/cond/branch_2_fun/ppermute | solution.py:283
  22.5 92.3 %collective-permute-start.12 = (bf16[80,2560]{1,0:T(8,128)(2,1)S(1)}, bf16[80,2560]{1,0:T(8,128)(2,1)S(1)}, u32[]{:S(2)}, u32[]{:S(2)}) collective-permute-start(bf16[80,2560]{1,0:T(8,128)(2,1)S(1)} %slice.51), channel_id=1, source_target_pairs={{0,16},{4,20},{8,24},{12,28},{16,32},{20,36},{24,40},{28,44},{32,4... | collective-permute-start | bytes 1228808 | tf_op jit(solution)/shard_map/cond/branch_2_fun/ppermute | solution.py:283
  41.2 21.0 %collective-permute-start.17 = (bf16[144,2560]{1,0:T(8,128)(2,1)}, bf16[144,2560]{1,0:T(8,128)(2,1)}, u32[]{:S(2)}, u32[]{:S(2)}) collective-permute-start(bf16[144,2560]{1,0:T(8,128)(2,1)} %collective-permute-done.15), channel_id=1, source_target_pairs={{0,48},{4,52},{8,56},{12,60},{16,0},{20,4},{24,8},{28,12},{32,80},... | collective-permute-start | bytes 2211848 | tf_op jit(solution)/shard_map/cond/branch_2_fun/ppermute | solution.py:338
  44.9 34.8 %collective-permute-start.16 = (bf16[160,2560]{1,0:T(8,128)(2,1)}, bf16[160,2560]{1,0:T(8,128)(2,1)}, u32[]{:S(2)}, u32[]{:S(2)}) collective-permute-start(bf16[160,2560]{1,0:T(8,128)(2,1)} %collective-permute-done.14), channel_id=1, source_target_pairs={{0,48},{4,52},{8,56},{12,60},{16,0},{20,4},{24,8},{28,12},{32,80},... | collective-permute-start | bytes 2457608 | tf_op jit(solution)/shard_map/cond/branch_2_fun/ppermute | solution.py:339
  44.9 38.5 %copy-start.2 = (bf16[1,640,2560]{2,1,0:T(8,128)(2,1)S(1)}, bf16[1,640,2560]{2,1,0:T(8,128)(2,1)}, u32[]{:S(2)}) copy-start(bf16[1,640,2560]{2,1,0:T(8,128)(2,1)} %get-tuple-element.70) | copy-start | bytes 9830404 | tf_op jit(solution)/shard_map/cond
  44.9 38.5 %copy-start.11 = (bf16[1,640,2560]{2,1,0:T(8,128)(2,1)S(1)}, bf16[1,640,2560]{2,1,0:T(8,128)(2,1)}, u32[]{:S(2)}) copy-start(bf16[1,640,2560]{2,1,0:T(8,128)(2,1)} %get-tuple-element.73) | copy-start | bytes 9830404 | tf_op jit(solution)/shard_map/cond
  44.9 38.5 %copy-start.16 = (f32[1,640]{1,0:T(1,128)S(1)}, f32[1,640]{1,0:T(1,128)}, u32[]{:S(2)}) copy-start(f32[1,640]{1,0:T(1,128)} %get-tuple-element.78.second_ref) | copy-start | bytes 7684 | tf_op jit(solution)/shard_map/cond
  62.1 43.6 %collective-permute-start.20 = (bf16[144,2560]{1,0:T(8,128)(2,1)}, bf16[144,2560]{1,0:T(8,128)(2,1)S(1)}, u32[]{:S(2)}, u32[]{:S(2)}) collective-permute-start(bf16[144,2560]{1,0:T(8,128)(2,1)} %collective-permute-done.17), channel_id=1, source_target_pairs={{0,48},{4,52},{8,56},{12,60},{16,0},{20,4},{24,8},{28,12},{32,16},... | collective-permute-start | bytes 2211848 | tf_op jit(solution)/shard_map/cond/branch_2_fun/ppermute | solution.py:340
  79.7 31.0 %collective-permute-start.18 = (bf16[160,2560]{1,0:T(8,128)(2,1)}, bf16[160,2560]{1,0:T(8,128)(2,1)S(1)}, u32[]{:S(2)}, u32[]{:S(2)}) collective-permute-start(bf16[160,2560]{1,0:T(8,128)(2,1)} %collective-permute-done.16), channel_id=1, source_target_pairs={{0,48},{4,52},{8,56},{12,60},{16,0},{20,4},{24,8},{28,12},{32,16},... | collective-permute-start | bytes 2457608 | tf_op jit(solution)/shard_map/cond/branch_2_fun/ppermute | solution.py:341

commit v3 on v2

--- a/solution.py
+++ b/solution.py
@@ -18,7 +18,7 @@
 BAND = 16
 TURNS = 4
 TOKS = 32
-SPLIT = (0, 9, 19, 35, 40)
+SPLIT = (0, 9, 19, 37, 40)
 
 
 def turn_pair(turns):
@@ -41,9 +41,8 @@
     return (jnp.where(cos_minus, -cos_size, cos_size), jnp.where(sin_minus, -sin_size, sin_size))
 
 
-def features_kernel(first_ref, codes_ref, feats_ref, change_ref, code_ref, band_ref, block_ref):
+def features_kernel(codes_ref, feats_ref, code_ref):
     tokens, width_all = feats_ref.shape
-    own_rows = change_ref.shape[0]
     root = math.sqrt(2.0)
     row = jnp.broadcast_to(codes_ref[...], (LANES, tokens))
 
@@ -75,6 +74,12 @@
 
     lax.fori_loop(0, tokens // TOKS, some_tokens, 0)
 
+
+def change_kernel(first_ref, codes_ref, change_ref, band_ref, block_ref):
+    own_rows, tokens = change_ref.shape
+    root = math.sqrt(2.0)
+    row = jnp.broadcast_to(codes_ref[...], (LANES, tokens))
+
     blocks = own_rows // BAND
     band = lax.broadcasted_iota(jnp.int32, (BAND, tokens), 0)
     block = lax.broadcasted_iota(jnp.int32, (blocks, tokens), 0)
@@ -90,7 +95,7 @@
         one = pl.ds(a, 1)
         here, there = (
             (block_ref[k, one, :] * band_ref[k] - block_ref[k + 1, one, :] * band_ref[k + 1])
-            .astype(feats_ref.dtype)
+            .astype(jnp.bfloat16)
             .astype(jnp.float32)
             for k in (0, 2)
         )
@@ -100,31 +105,40 @@
     lax.fori_loop(0, blocks, some_rows, 0, unroll=4)
 
 
-def make_features(codes, first_col, tok_rows, own_rows, width_all):
-    count = codes.shape[0]
+def make_features(codes, width_all):
+    count, tok_rows = codes.shape
     return pl.pallas_call(
         features_kernel,
         grid=(count,),
-        out_shape=(
-            jax.ShapeDtypeStruct((count * tok_rows, width_all), jnp.bfloat16),
-            jax.ShapeDtypeStruct((own_rows, count * tok_rows), jnp.float32),
+        out_shape=jax.ShapeDtypeStruct((count * tok_rows, width_all), jnp.bfloat16),
+        in_specs=[pl.BlockSpec((None, 1, tok_rows), lambda s: (s, 0, 0))],
+        out_specs=pl.BlockSpec((tok_rows, width_all), lambda s: (s, 0)),
+        scratch_shapes=[pltpu.VMEM((tok_rows, LANES), jnp.int32)],
+        compiler_params=pltpu.CompilerParams(vmem_limit_bytes=12 * 2**20),
+        cost_estimate=pl.CostEstimate(
+            flops=4 * 10**9, bytes_accessed=5 * 2**20, transcendentals=0
         ),
+    )(codes[:, None, :])
+
+
+def make_change(codes, first_col, own_rows):
+    count, tok_rows = codes.shape
+    return pl.pallas_call(
+        change_kernel,
+        grid=(count,),
+        out_shape=jax.ShapeDtypeStruct((own_rows, count * tok_rows), jnp.float32),
         in_specs=[
             pl.BlockSpec(memory_space=pltpu.SMEM),
             pl.BlockSpec((None, 1, tok_rows), lambda s: (s, 0, 0)),
         ],
-        out_specs=(
-            pl.BlockSpec((tok_rows, width_all), lambda s: (s, 0)),
-            pl.BlockSpec((own_rows, tok_rows), lambda s: (0, s)),
-        ),
+        out_specs=pl.BlockSpec((own_rows, tok_rows), lambda s: (0, s)),
         scratch_shapes=[
-            pltpu.VMEM((tok_rows, LANES), jnp.int32),
             pltpu.VMEM((4, BAND, tok_rows), jnp.float32),
             pltpu.VMEM((4, own_rows // BAND, tok_rows), jnp.float32),
         ],
         compiler_params=pltpu.CompilerParams(vmem_limit_bytes=12 * 2**20),
         cost_estimate=pl.CostEstimate(
-            flops=9 * 10**9, bytes_accessed=8 * 2**20, transcendentals=0
+            flops=4 * 10**9, bytes_accessed=3 * 2**20, transcendentals=0
         ),
     )(first_col.reshape(1), codes[:, None, :])
 
@@ -331,14 +345,18 @@
         )
     first_col = lax.axis_index("fsdp") * own_rows
     mom_far = []
-    feats, change = make_features(codes, first_col, tok_rows, own_rows, width_all)
     if relay:
         first, second_hop, last = long_way(distance, lax.axis_size("dp"))
         one, two = (lax.ppermute(part, "dp", first) for part in mom_own_parts[:2])
-        one_next = lax.ppermute(one, "dp", second_hop)
-        two_next = lax.ppermute(after(two, one), "dp", second_hop)
-        mom_far.append(lax.ppermute(one_next, "dp", last))
-        mom_far.append(lax.ppermute(after(two_next, one_next, feats, change), "dp", last))
+        feats = make_features(after(codes, one), width_all)
+        one = lax.ppermute(one, "dp", second_hop)
+        two = lax.ppermute(after(two, feats), "dp", second_hop)
+        change = make_change(after(codes, one), first_col, own_rows)
+        mom_far.append(lax.ppermute(one, "dp", last))
+        mom_far.append(lax.ppermute(after(two, change), "dp", last))
+    else:
+        feats = make_features(codes, width_all)
+        change = make_change(codes, first_col, own_rows)
     for part in mom_own_parts[len(mom_far) :]:
         mom_far.append(turned(part, "dp", distance))
 
@@ -347,10 +365,7 @@
     )
     second_new, rate = columns[::order]
     outs = None
-    pieces = list(zip(starts, mom_far))
-    if relay:
-        pieces[1], pieces[2] = pieces[2], pieces[1]
-    for low, far in pieces:
+    for low, far in zip(starts, mom_far):
         outs = update(low, far, lead, mixed, rate, outs, order)
     param_new, mom_new = outs[::order]
     return (param_new[None], mom_new[None], second_new)

time: 115 us -> 115 us (level)
  waiting for transfers between devices: 43.9 us -> 24.4 us
  blocking collectives: 0 us -> 15.1 us
  starting transfers between devices: 25 us -> 29.2 us
    all_to_all x0 -> x1, blocking collectives: none -> 15.1 us  [step_at(): lax.all_to_all(jnp.broadcast_to(own_codes, (groups, tok_rows)), 'fsdp', 0...]
    ppermute x3, starting transfers between devices: 2.89 us -> 16.8 us  [turned(): lax.ppermute(value, axis, [(i, (i + by) % size) for i in range(size)])]
    ppermute x2, waiting for transfers between devices: 18.6 us -> 5.35 us  [step_at(): one, two = (lax.ppermute(part, 'dp', first) for part in mom_own_parts[:2])]
    all_to_all x1 -> x0, starting transfers between devices: 7.56 us -> none  [step_at(): lax.all_to_all(jnp.broadcast_to(own_codes, (groups, tok_rows)), 'fsdp', 0...]
    ppermute x4, waiting for transfers between devices: 23 us -> 16.7 us  [the longest x1 12.2 us: step_at(): two = lax.ppermute(after(two, feats), 'dp', second_hop)]
    cond x8 -> x13, local copies, waits for them, and re-layouts: 0.02 us -> 2.34 us
    ppermute x4, starting transfers between devices: 11.1 us -> 8.79 us  [the longest x1 3.8 us: step_at(): two = lax.ppermute(after(two, feats), 'dp', second_hop)]
    slice x4, local copies, waits for them, and re-layouts: 6.54 us -> 4.79 us  [step_at(): mom_own_parts.append(whole[low:high])]
  transfers between devices with their start and end apart: 10 -> 9, of which waited for: 4 -> 6; matrix products, arithmetic and copies ran while one was open for 6% -> 4% of each run, Pallas kernels for 32% -> 32%
where the time goes in v3:
time: 115 us; the launch traced here: 116 us
  Pallas kernels  38.4 us (33%)
  starting transfers between devices  29.2 us (25%)
  waiting for transfers between devices  24.4 us (21%)
  blocking collectives  15.1 us (13%)
  local copies, waits for them, and re-layouts  7.15 us (6%)
  between operations  1.29 us (1%)
    pallas_call x1, Pallas kernels, make_gradient(): pl.pallas_call(partial(gradient_kernel, order, tile), grid=(groups,), out...  22.4 us
    ppermute x3, starting transfers between devices, turned(): lax.ppermute(value, axis, [(i, (i + by) % size) for i in range(size)])  16.8 us
    all_to_all x1, blocking collectives, step_at(): lax.all_to_all(jnp.broadcast_to(own_codes, (groups, tok_rows)), 'fsdp', 0...  15.1 us
    ppermute x1, waiting for transfers between devices, step_at(): two = lax.ppermute(after(two, feats), 'dp', second_hop)  12.2 us
    pallas_call x4, Pallas kernels, update(): pl.pallas_call(partial(update_kernel, order), grid=(rows // block,), out_...  7.88 us
    pallas_call x1, Pallas kernels, make_features(): pl.pallas_call(features_kernel, grid=(count,), out_shape=jax.ShapeDtypeSt...  6.07 us
    ppermute x2, waiting for transfers between devices, step_at(): one, two = (lax.ppermute(part, 'dp', first) for part in mom_own_parts[:2])  5.35 us
    slice x4, local copies, waits for them, and re-layouts, step_at(): mom_own_parts.append(whole[low:high])  4.79 us
  transfers between devices with their start and end apart: 9, of which 6 were waited for; matrix products, arithmetic and copies ran while one was open for 4% of the time, Pallas kernels for 32%

profile of v3, /device:TPU:32, one launch (start us, length us, event | category | flops | bytes accessed | tf_op | source)
XLA Modules:
  0.0 115.8 jit_solution(9131932680813896340)
XLA Ops:
  1.3 114.5 %conditional.1 = (f32[1,640]{1,0:T(1,128)}, bf16[640,2560]{1,0:T(8,128)(2,1)}, bf16[640,2560]{1,0:T(8,128)(2,1)}) conditional(s32[]{:T(128)} %clamp.3, (bf16[1,640,2560]{2,1,0:T(8,128)(2,1)}, bf16[1,640,2560]{2,1,0:T(8,128)(2,1)}, s32[1,256]{1,0:T(1,128)}, f32[1,640]{1,0:T(1,128)}) %tuple.44, ...), branch_computations={%region_0.1_spmd, %region_1.2_spmd, %region_2.3_spmd, %region_3.4_... | conditional | flops 38009835520 | bytes 172936736 | solution.py:377
  1.5 0.0 copy-start.11
  1.5 1.7 %collective-permute-start.13 = (bf16[640,2560]{1,0:T(8,128)(2,1)}, bf16[640,2560]{1,0:T(8,128)(2,1)}, u32[]{:S(2)}, u32[]{:S(2)}) collective-permute-start(bf16[640,2560]{1,0:T(8,128)(2,1)} %bitcast.64), channel_id=1, source_target_pairs={{0,16},{4,20},{8,24},{12,28},{16,32},{20,36},{24,40},{28,44},{32,4... | collective-permute-start | bytes 9830408 | tf_op jit(solution)/shard_map/cond/branch_2_fun/ppermute | solution.py:297
  3.2 1.2 %slice_bitcast_fusion.3 = bf16[144,2560]{1,0:T(8,128)(2,1)S(1)} fusion(bf16[1,640,2560]{2,1,0:T(8,128)(2,1)} %get-tuple-element.66), kind=kLoop, calls=%fused_computation.5 | loop fusion | bytes 1474560 | tf_op jit(solution)/shard_map/cond/branch_2_fun/slice | solution.py:336
  4.3 2.7 %collective-permute-start.14 = (bf16[144,2560]{1,0:T(8,128)(2,1)S(1)}, bf16[144,2560]{1,0:T(8,128)(2,1)}, u32[]{:S(2)}, u32[]{:S(2)}) collective-permute-start(bf16[144,2560]{1,0:T(8,128)(2,1)S(1)} %slice_bitcast_fusion.3), channel_id=1, source_target_pairs={{0,48},{4,52},{8,56},{12,60},{16,0},{20,4},{24,8},{28,12},{32,16},... | collective-permute-start | bytes 2211848 | tf_op jit(solution)/shard_map/cond/branch_2_fun/ppermute | solution.py:350
  7.0 1.2 %slice_bitcast_fusion.2 = bf16[160,2560]{1,0:T(8,128)(2,1)S(1)} fusion(bf16[1,640,2560]{2,1,0:T(8,128)(2,1)} %get-tuple-element.66), kind=kLoop, calls=%fused_computation.4 | loop fusion | bytes 1638400 | tf_op jit(solution)/shard_map/cond/branch_2_fun/slice | solution.py:336
  8.2 1.0 collective-permute-start.17
  9.1 1.5 %slice.50 = bf16[288,2560]{1,0:T(8,128)(2,1)S(1)} slice(bf16[640,2560]{1,0:T(8,128)(2,1)} %bitcast.47), slice={[304:592], [0:2560]} | slice | bytes 2949120 | tf_op jit(solution)/shard_map/cond/branch_2_fun/slice | solution.py:336
  10.6 0.0 copy-done.11
  10.6 15.1 %all_to_all.19 = s32[4,1,256]{2,1,0:T(1,128)S(1)} all-to-all(s32[4,1,256]{2,1,0:T(1,128)S(1)} %broadcast_in_dim.48), channel_id=1, replica_groups=mesh['dp'=64,'fsdp'=4] {'fsdp'}, dimensions={0} | all-to-all | bytes 8192 | tf_op jit(solution)/shard_map/cond/branch_2_fun/all_to_all | solution.py:343
  25.7 0.0 collective-permute-done.14
  25.7 2.0 %collective-permute-start.15 = (bf16[144,2560]{1,0:T(8,128)(2,1)}, bf16[144,2560]{1,0:T(8,128)(2,1)}, u32[]{:S(2)}, u32[]{:S(2)}) collective-permute-start(bf16[144,2560]{1,0:T(8,128)(2,1)} %collective-permute-done.14), channel_id=1, source_target_pairs={{0,48},{4,52},{8,56},{12,60},{16,0},{20,4},{24,8},{28,12},{32,80},... | collective-permute-start | bytes 2211848 | tf_op jit(solution)/shard_map/cond/branch_2_fun/ppermute | solution.py:352
  27.7 6.1 %branch_2_fun.7.feats_ref = bf16[1024,2560]{1,0:T(8,128)(2,1)S(1)} custom-call(s32[4,1,256]{2,1,0:T(1,128)S(1)} %copy.28.codes_ref), custom_call_target="tpu_custom_call" | custom-call | flops 4000000000 | bytes 5242880 | tf_op jit(solution)/shard_map/cond/branch_2_fun/pallas_call | solution.py:110
  33.8 0.0 copy-start
  33.8 2.3 %copy-done = bf16[1024,2560]{1,0:T(8,128)(2,1)} copy-done((bf16[1024,2560]{1,0:T(8,128)(2,1)}, bf16[1024,2560]{1,0:T(8,128)(2,1)S(1)}, u32[]{:S(2)}) %copy-start) | copy-done | bytes 5242904 | tf_op jit(solution)/shard_map/cond
  36.1 5.3 %collective-permute-done.17 = bf16[160,2560]{1,0:T(8,128)(2,1)} collective-permute-done((bf16[160,2560]{1,0:T(8,128)(2,1)S(1)}, bf16[160,2560]{1,0:T(8,128)(2,1)}, u32[]{:S(2)}, u32[]{:S(2)}) %collective-permute-start.17) | collective-permute-done | bytes 819232 | tf_op jit(solution)/shard_map/cond/branch_2_fun/ppermute | solution.py:350
  41.5 3.8 %collective-permute-start.18 = (bf16[160,2560]{1,0:T(8,128)(2,1)}, bf16[160,2560]{1,0:T(8,128)(2,1)}, u32[]{:S(2)}, u32[]{:S(2)}) collective-permute-start(bf16[160,2560]{1,0:T(8,128)(2,1)} %collective-permute-done.17), channel_id=1, source_target_pairs={{0,48},{4,52},{8,56},{12,60},{16,0},{20,4},{24,8},{28,12},{32,80},... | collective-permute-start | bytes 2457608 | tf_op jit(solution)/shard_map/cond/branch_2_fun/ppermute | solution.py:353
  45.3 12.1 %collective-permute-start.16 = (bf16[288,2560]{1,0:T(8,128)(2,1)S(1)}, bf16[288,2560]{1,0:T(8,128)(2,1)S(1)}, u32[]{:S(2)}, u32[]{:S(2)}) collective-permute-start(bf16[288,2560]{1,0:T(8,128)(2,1)S(1)} %slice.50), channel_id=1, source_target_pairs={{0,16},{4,20},{8,24},{12,28},{16,32},{20,36},{24,40},{28,44},{32,4... | collective-permute-start | bytes 4423688 | tf_op jit(solution)/shard_map/cond/branch_2_fun/ppermute | solution.py:297
  57.4 1.0 slice.51
  58.4 3.0 %collective-permute-start.12 = (bf16[48,2560]{1,0:T(8,128)(2,1)S(1)}, bf16[48,2560]{1,0:T(8,128)(2,1)S(1)}, u32[]{:S(2)}, u32[]{:S(2)}) collective-permute-start(bf16[48,2560]{1,0:T(8,128)(2,1)S(1)} %slice.51), channel_id=1, source_target_pairs={{0,16},{4,20},{8,24},{12,28},{16,32},{20,36},{24,40},{28,44},{32,4... | collective-permute-start | bytes 737288 | tf_op jit(solution)/shard_map/cond/branch_2_fun/ppermute | solution.py:297
  61.4 0.0 collective-permute-done.15
  61.4 1.2 %collective-permute-start.20 = (bf16[144,2560]{1,0:T(8,128)(2,1)}, bf16[144,2560]{1,0:T(8,128)(2,1)S(1)}, u32[]{:S(2)}, u32[]{:S(2)}) collective-permute-start(bf16[144,2560]{1,0:T(8,128)(2,1)} %collective-permute-done.15), channel_id=1, source_target_pairs={{0,48},{4,52},{8,56},{12,60},{16,0},{20,4},{24,8},{28,12},{32,16},... | collective-permute-start | bytes 2211848 | tf_op jit(solution)/shard_map/cond/branch_2_fun/ppermute | solution.py:355
  62.6 0.0 copy-start.1
  62.6 0.0 copy-start.6
  62.6 0.0 copy-start.15
  62.6 0.0 copy-start.20
  62.6 2.0 %branch_2_fun.8.change_ref = f32[640,1024]{1,0:T(8,128)S(1)} custom-call(s32[1]{0:T(128)} %bitcast.14.first_ref, s32[4,1,256]{2,1,0:T(1,128)S(1)} %broadcast_in_dim.50.codes_ref), custom_call_target="tpu_custom_call" | custom-call | flops 4000000000 | bytes 3145728 | tf_op jit(solution)/shard_map/cond/branch_2_fun/pallas_call | solution.py:126
  64.7 12.2 %collective-permute-done.18 = bf16[160,2560]{1,0:T(8,128)(2,1)} collective-permute-done((bf16[160,2560]{1,0:T(8,128)(2,1)}, bf16[160,2560]{1,0:T(8,128)(2,1)}, u32[]{:S(2)}, u32[]{:S(2)}) %collective-permute-start.18) | collective-permute-done | bytes 819232 | tf_op jit(solution)/shard_map/cond/branch_2_fun/ppermute | solution.py:353
  76.9 1.8 %collective-permute-start.19 = (bf16[160,2560]{1,0:T(8,128)(2,1)}, bf16[160,2560]{1,0:T(8,128)(2,1)S(1)}, u32[]{:S(2)}, u32[]{:S(2)}) collective-permute-start(bf16[160,2560]{1,0:T(8,128)(2,1)} %collective-permute-done.18), channel_id=1, source_target_pairs={{0,48},{4,52},{8,56},{12,60},{16,0},{20,4},{24,8},{28,12},{32,16},... | collective-permute-start | bytes 2457608 | tf_op jit(solution)/shard_map/cond/branch_2_fun/ppermute | solution.py:356
  78.6 0.4 collective-permute-done.13.far_ref
  79.0 0.0 copy-done.1
  79.0 0.0 copy-done.6
  79.0 0.0 copy-done.15
  79.0 0.0 copy-done.20
  79.0 22.4 %branch_2_fun.9 = (bf16[640,2560]{1,0:T(8,128)(2,1)S(1)}, f32[640,2560]{1,0:T(8,128)S(1)}, f32[1,640]{1,0:T(1,128)}, f32[640,1]{1,0:T(8,128)S(1)}) custom-call(bf16[640,2560]{1,0:T(8,128)(2,1)S(1)} %bitcast.65, bf16[640,2560]{1,0:T(8,128)(2,1)} %collective-permute-done.13.far_ref, bf16[1024,2560]{1,0:T(8,128)(2,1)S(1)} %copy-done.1, ...), custom_call_target="tpu_custom_call" | custom-call | flops 30000001024 | bytes 31457280 | tf_op jit(solution)/shard_map/cond/branch_2_fun/pallas_call | solution.py:229
  101.4 0.0 collective-permute-done.20.far_ref
  101.4 2.1 %branch_2_fun.10 = (bf16[640,2560]{1,0:T(8,128)(2,1)}, bf16[640,2560]{1,0:T(8,128)(2,1)}) custom-call(bf16[144,2560]{1,0:T(8,128)(2,1)S(1)} %collective-permute-done.20.far_ref, f32[640,2560]{1,0:T(8,128)S(1)} %get-tuple-element.75.lead_ref, bf16[640,2560]{1,0:T(8,128)(2,1)S(1)} %get-tuple-element.76.mixed_ref, f32[640,1]{1,0:T(8,128)S(1)} %get-tuple-element.77.rate_ref), custom_call_target="tpu_custom_call" | custom-call | flops 2211840 | bytes 4423680 | tf_op jit(solution)/shard_map/cond/branch_2_fun/pallas_call | solution.py:280
  103.5 4.5 %collective-permute-done.19.far_ref = bf16[160,2560]{1,0:T(8,128)(2,1)S(1)} collective-permute-done((bf16[160,2560]{1,0:T(8,128)(2,1)}, bf16[160,2560]{1,0:T(8,128)(2,1)S(1)}, u32[]{:S(2)}, u32[]{:S(2)}) %collective-permute-start.19) | collective-permute-done | bytes 819232 | tf_op jit(solution)/shard_map/cond/branch_2_fun/ppermute | solution.py:356
  108.0 1.8 %branch_2_fun.11 = (bf16[640,2560]{1,0:T(8,128)(2,1)}, bf16[640,2560]{1,0:T(8,128)(2,1)}) custom-call(bf16[160,2560]{1,0:T(8,128)(2,1)S(1)} %collective-permute-done.19.far_ref, f32[640,2560]{1,0:T(8,128)S(1)} %get-tuple-element.75.lead_ref, bf16[640,2560]{1,0:T(8,128)(2,1)S(1)} %get-tuple-element.76.mixed_ref, ...), custom_call_target="tpu_custom_call", output_to_operand_aliasing={{0}: (4, {}), {1}: (5, {})} | custom-call | flops 2457600 | bytes 4915200 | tf_op jit(solution)/shard_map/cond/branch_2_fun/pallas_call | solution.py:280
  109.8 0.7 collective-permute-done.16.far_ref
  110.5 3.0 %branch_2_fun.12 = (bf16[640,2560]{1,0:T(8,128)(2,1)}, bf16[640,2560]{1,0:T(8,128)(2,1)}) custom-call(bf16[288,2560]{1,0:T(8,128)(2,1)S(1)} %collective-permute-done.16.far_ref, f32[640,2560]{1,0:T(8,128)S(1)} %get-tuple-element.75.lead_ref, bf16[640,2560]{1,0:T(8,128)(2,1)S(1)} %get-tuple-element.76.mixed_ref, ...), custom_call_target="tpu_custom_call", output_to_operand_aliasing={{0}: (4, {}), {1}: (5, {})} | custom-call | flops 4423680 | bytes 8847360 | tf_op jit(solution)/shard_map/cond/branch_2_fun/pallas_call | solution.py:280
  113.5 1.3 %collective-permute-done.12.far_ref = bf16[48,2560]{1,0:T(8,128)(2,1)S(1)} collective-permute-done((bf16[48,2560]{1,0:T(8,128)(2,1)S(1)}, bf16[48,2560]{1,0:T(8,128)(2,1)S(1)}, u32[]{:S(2)}, u32[]{:S(2)}) %collective-permute-start.12) | collective-permute-done | bytes 245792 | tf_op jit(solution)/shard_map/cond/branch_2_fun/ppermute | solution.py:297
  114.8 1.0 branch_2_fun.13
  (4 shorter events, 0.0 us)
Async XLA Ops:
  1.5 9.1 %copy-start.11 = (s32[1,256]{1,0:T(1,128)S(1)}, s32[1,256]{1,0:T(1,128)}, u32[]{:S(2)}) copy-start(s32[1,256]{1,0:T(1,128)} %get-tuple-element.71) | copy-start | bytes 3076 | tf_op jit(solution)/shard_map/cond
  1.5 77.5 %collective-permute-start.13 = (bf16[640,2560]{1,0:T(8,128)(2,1)}, bf16[640,2560]{1,0:T(8,128)(2,1)}, u32[]{:S(2)}, u32[]{:S(2)}) collective-permute-start(bf16[640,2560]{1,0:T(8,128)(2,1)} %bitcast.64), channel_id=1, source_target_pairs={{0,16},{4,20},{8,24},{12,28},{16,32},{20,36},{24,40},{28,44},{32,4... | collective-permute-start | bytes 9830408 | tf_op jit(solution)/shard_map/cond/branch_2_fun/ppermute | solution.py:297
  4.3 21.4 %collective-permute-start.14 = (bf16[144,2560]{1,0:T(8,128)(2,1)S(1)}, bf16[144,2560]{1,0:T(8,128)(2,1)}, u32[]{:S(2)}, u32[]{:S(2)}) collective-permute-start(bf16[144,2560]{1,0:T(8,128)(2,1)S(1)} %slice_bitcast_fusion.3), channel_id=1, source_target_pairs={{0,48},{4,52},{8,56},{12,60},{16,0},{20,4},{24,8},{28,12},{32,16},... | collective-permute-start | bytes 2211848 | tf_op jit(solution)/shard_map/cond/branch_2_fun/ppermute | solution.py:350
  8.2 33.3 %collective-permute-start.17 = (bf16[160,2560]{1,0:T(8,128)(2,1)S(1)}, bf16[160,2560]{1,0:T(8,128)(2,1)}, u32[]{:S(2)}, u32[]{:S(2)}) collective-permute-start(bf16[160,2560]{1,0:T(8,128)(2,1)S(1)} %slice_bitcast_fusion.2), channel_id=1, source_target_pairs={{0,48},{4,52},{8,56},{12,60},{16,0},{20,4},{24,8},{28,12},{32,16},... | collective-permute-start | bytes 2457608 | tf_op jit(solution)/shard_map/cond/branch_2_fun/ppermute | solution.py:350
  25.7 35.7 %collective-permute-start.15 = (bf16[144,2560]{1,0:T(8,128)(2,1)}, bf16[144,2560]{1,0:T(8,128)(2,1)}, u32[]{:S(2)}, u32[]{:S(2)}) collective-permute-start(bf16[144,2560]{1,0:T(8,128)(2,1)} %collective-permute-done.14), channel_id=1, source_target_pairs={{0,48},{4,52},{8,56},{12,60},{16,0},{20,4},{24,8},{28,12},{32,80},... | collective-permute-start | bytes 2211848 | tf_op jit(solution)/shard_map/cond/branch_2_fun/ppermute | solution.py:352
  33.8 2.3 %copy-start = (bf16[1024,2560]{1,0:T(8,128)(2,1)}, bf16[1024,2560]{1,0:T(8,128)(2,1)S(1)}, u32[]{:S(2)}) copy-start(bf16[1024,2560]{1,0:T(8,128)(2,1)S(1)} %branch_2_fun.7.feats_ref) | copy-start | bytes 15728644 | tf_op jit(solution)/shard_map/cond
  41.5 35.4 %collective-permute-start.18 = (bf16[160,2560]{1,0:T(8,128)(2,1)}, bf16[160,2560]{1,0:T(8,128)(2,1)}, u32[]{:S(2)}, u32[]{:S(2)}) collective-permute-start(bf16[160,2560]{1,0:T(8,128)(2,1)} %collective-permute-done.17), channel_id=1, source_target_pairs={{0,48},{4,52},{8,56},{12,60},{16,0},{20,4},{24,8},{28,12},{32,80},... | collective-permute-start | bytes 2457608 | tf_op jit(solution)/shard_map/cond/branch_2_fun/ppermute | solution.py:353
  45.3 65.2 %collective-permute-start.16 = (bf16[288,2560]{1,0:T(8,128)(2,1)S(1)}, bf16[288,2560]{1,0:T(8,128)(2,1)S(1)}, u32[]{:S(2)}, u32[]{:S(2)}) collective-permute-start(bf16[288,2560]{1,0:T(8,128)(2,1)S(1)} %slice.50), channel_id=1, source_target_pairs={{0,16},{4,20},{8,24},{12,28},{16,32},{20,36},{24,40},{28,44},{32,4... | collective-permute-start | bytes 4423688 | tf_op jit(solution)/shard_map/cond/branch_2_fun/ppermute | solution.py:297
  58.4 56.4 %collective-permute-start.12 = (bf16[48,2560]{1,0:T(8,128)(2,1)S(1)}, bf16[48,2560]{1,0:T(8,128)(2,1)S(1)}, u32[]{:S(2)}, u32[]{:S(2)}) collective-permute-start(bf16[48,2560]{1,0:T(8,128)(2,1)S(1)} %slice.51), channel_id=1, source_target_pairs={{0,16},{4,20},{8,24},{12,28},{16,32},{20,36},{24,40},{28,44},{32,4... | collective-permute-start | bytes 737288 | tf_op jit(solution)/shard_map/cond/branch_2_fun/ppermute | solution.py:297
  61.4 40.0 %collective-permute-start.20 = (bf16[144,2560]{1,0:T(8,128)(2,1)}, bf16[144,2560]{1,0:T(8,128)(2,1)S(1)}, u32[]{:S(2)}, u32[]{:S(2)}) collective-permute-start(bf16[144,2560]{1,0:T(8,128)(2,1)} %collective-permute-done.15), channel_id=1, source_target_pairs={{0,48},{4,52},{8,56},{12,60},{16,0},{20,4},{24,8},{28,12},{32,16},... | collective-permute-start | bytes 2211848 | tf_op jit(solution)/shard_map/cond/branch_2_fun/ppermute | solution.py:355
  62.6 16.4 %copy-start.1 = (bf16[1024,2560]{1,0:T(8,128)(2,1)S(1)}, bf16[1024,2560]{1,0:T(8,128)(2,1)}, u32[]{:S(2)}) copy-start(bf16[1024,2560]{1,0:T(8,128)(2,1)} %copy-done) | copy-start | bytes 15728644 | tf_op jit(solution)/shard_map/cond
  62.6 16.4 %copy-start.6 = (bf16[1,640,2560]{2,1,0:T(8,128)(2,1)S(1)}, bf16[1,640,2560]{2,1,0:T(8,128)(2,1)}, u32[]{:S(2)}) copy-start(bf16[1,640,2560]{2,1,0:T(8,128)(2,1)} %get-tuple-element.66) | copy-start | bytes 9830404 | tf_op jit(solution)/shard_map/cond
  62.6 16.4 %copy-start.15 = (bf16[1,640,2560]{2,1,0:T(8,128)(2,1)S(1)}, bf16[1,640,2560]{2,1,0:T(8,128)(2,1)}, u32[]{:S(2)}) copy-start(bf16[1,640,2560]{2,1,0:T(8,128)(2,1)} %get-tuple-element.69) | copy-start | bytes 9830404 | tf_op jit(solution)/shard_map/cond
  62.6 16.4 %copy-start.20 = (f32[1,640]{1,0:T(1,128)S(1)}, f32[1,640]{1,0:T(1,128)}, u32[]{:S(2)}) copy-start(f32[1,640]{1,0:T(1,128)} %get-tuple-element.74.second_ref) | copy-start | bytes 7684 | tf_op jit(solution)/shard_map/cond
  76.9 31.1 %collective-permute-start.19 = (bf16[160,2560]{1,0:T(8,128)(2,1)}, bf16[160,2560]{1,0:T(8,128)(2,1)S(1)}, u32[]{:S(2)}, u32[]{:S(2)}) collective-permute-start(bf16[160,2560]{1,0:T(8,128)(2,1)} %collective-permute-done.18), channel_id=1, source_target_pairs={{0,48},{4,52},{8,56},{12,60},{16,0},{20,4},{24,8},{28,12},{32,16},... | collective-permute-start | bytes 2457608 | tf_op jit(solution)/shard_map/cond/branch_2_fun/ppermute | solution.py:356
